TPU v7x, 512 devices: a whole 4x4x16 slice. The times are simulated.
512 devices in a mesh: gx: 4 (over y), gy: 16 (over z), gz: 8 (over x, core).
Axes of the slice: x: 4, y: 4, z: 16, core: 2. Of those that a mesh axis runs over, the one named last changes fastest.
Arguments:
- right_side: float32 [64, 128, 512], P('gz', 'gy', 'gx'), may hold values from -6 to 6
- perm_class: int32 [64, 128, 512], P('gz', 'gy', 'gx'), may hold values from 0 to 15
- class_perm: float32 [16], replicated, may hold values from 0.1 to 10
- class_store: float32 [16], replicated, may hold values from 0.2 to 2
- coarse_basis: bfloat16 [32, 64, 128, 512], P(None, 'gz', 'gy', 'gx'), may hold values from -1 to 1
- brick_owner: int32 [8, 16, 4], P('gz', 'gy', 'gx'), may hold values from 0 to 7
- coarse_inverse: float32 [256, 256], replicated, as said below
Outputs:
- solution_field: float32 [64, 128, 512], P('gz', 'gy', 'gx')
Inputs may be any that keep to these rules, and one draw needn't show every extreme that they name: `coarse_inverse`: symmetric; each diagonal entry exceeds the sum of the magnitudes of the other entries of its row.
All inputs are finite; a program needn't handle non-finite values.
Results may differ from a plain program's by a relative error of at most 0.0054.
Values sent between devices are 32-bit elements; how exact they have to be, the bound alone decides.
No kernel may reach another device: no remote copies, remote signals or barrier semaphores. Data moves between devices by JAX's collectives and lax.ppermute only.
A program may use at most 64 MiB of HBM per device.

v0:
```python
import jax
import jax.numpy as jnp
from jax import lax
from jax.sharding import PartitionSpec as P

SWEEPS = 4
ITERS = 3


relaxation = 0.6


def with_halo(shard, sides, width):
    for axis, dim in sides:
        size, length = (lax.axis_size(axis), shard.shape[dim])
        up = [(i, (i + 1) % size) for i in range(size - 1)]
        down = [(j, i) for i, j in up]
        last = lax.slice_in_dim(shard, length - width, length, axis=dim)
        first = lax.slice_in_dim(shard, 0, width, axis=dim)
        before = lax.ppermute(last, axis, up)
        after = lax.ppermute(first, axis, down)
        shard = jnp.concatenate([before, shard, after], axis=dim)
    return shard


def harmonic(near_value, far_value):
    total = near_value + far_value
    return 2.0 * near_value * far_value / jnp.where(total > 0, total, 1.0)


def neighbours(padded):
    middle = padded[1:-1, 1:-1, 1:-1]
    beside_all = (
        padded[:-2, 1:-1, 1:-1],
        padded[2:, 1:-1, 1:-1],
        padded[1:-1, :-2, 1:-1],
        padded[1:-1, 2:, 1:-1],
        padded[1:-1, 1:-1, :-2],
        padded[1:-1, 1:-1, 2:],
    )
    return (middle, beside_all)


def operate(field, storage, trans_list):
    padded = with_halo(field, (("gx", 2), ("gy", 1), ("gz", 0)), 1)
    middle, beside_all = neighbours(padded)
    result = storage * middle
    for face_trans, beside in zip(trans_list, beside_all):
        result = result + face_trans * (middle - beside)
    return result


def local_sweeps(residual, diagonal, storage, trans_list):
    smooth = residual / diagonal
    for sweep_index in range(SWEEPS - 1):
        smooth = smooth + relaxation * (residual - operate(smooth, storage, trans_list)) / diagonal
    return smooth


def precondition(residual, diagonal, storage, trans_list, basis_flat, owner_mask, coarse_inverse):
    basis_count = basis_flat.shape[0]
    resid_low = residual.astype(jnp.bfloat16).reshape(-1)
    projected = jnp.dot(basis_flat, resid_low, preferred_element_type=jnp.float32)
    local_coarse = (owner_mask[:, None] * projected[None, :]).reshape(-1)
    coarse = lax.psum(local_coarse, ("gx", "gy", "gz"))
    smooth = local_sweeps(residual, diagonal, storage, trans_list)
    local_inner = jnp.sum(residual * smooth)
    inner_part = lax.psum(local_inner, ("gx", "gy", "gz"))
    coarse_value = jnp.dot(coarse_inverse, coarse, precision=lax.Precision.HIGHEST)
    value_low = coarse_value.astype(jnp.bfloat16)
    inner_now = inner_part + jnp.sum(coarse * value_low.astype(jnp.float32))
    owners = owner_mask.shape[0]
    mine = jnp.dot(
        owner_mask,
        value_low.astype(jnp.float32).reshape(owners, basis_count),
        precision=lax.Precision.HIGHEST,
    ).astype(jnp.bfloat16)
    correction = jnp.dot(mine, basis_flat, preferred_element_type=jnp.float32)
    return (smooth + correction.reshape(residual.shape), inner_now)


def on_device(
    right_side, perm_class, class_perm, class_store, coarse_basis, brick_owner, coarse_inverse
):
    classes = class_perm.shape[0]
    class_mask = perm_class[None] == jnp.arange(classes, dtype=jnp.int32)[:, None, None, None]
    conduct = jnp.sum(jnp.where(class_mask, class_perm[:, None, None, None], 0.0), axis=0)
    storage = jnp.sum(jnp.where(class_mask, class_store[:, None, None, None], 0.0), axis=0)
    padded = with_halo(conduct, (("gx", 2), ("gy", 1), ("gz", 0)), 1)
    middle, beside_all = neighbours(padded)
    trans_list = tuple((harmonic(middle, beside) for beside in beside_all))
    diagonal = storage
    for face_trans in trans_list:
        diagonal = diagonal + face_trans
    basis_flat = coarse_basis.reshape(coarse_basis.shape[0], -1)
    owners = coarse_inverse.shape[0] // coarse_basis.shape[0]
    owner_mask = (brick_owner.reshape(()) == jnp.arange(owners, dtype=jnp.int32)).astype(
        jnp.float32
    )
    solution_field = jnp.zeros_like(right_side)
    residual = right_side
    precond, inner_now = precondition(
        residual, diagonal, storage, trans_list, basis_flat, owner_mask, coarse_inverse
    )
    direction = precond
    for iteration in range(ITERS):
        image = operate(direction, storage, trans_list)
        step_size = inner_now / lax.psum(jnp.sum(direction * image), ("gx", "gy", "gz"))
        solution_field = solution_field + step_size * direction
        residual = residual - step_size * image
        if iteration + 1 < ITERS:
            precond, inner_next = precondition(
                residual, diagonal, storage, trans_list, basis_flat, owner_mask, coarse_inverse
            )
            ratio_next = inner_next / inner_now
            direction = precond + ratio_next * direction
            inner_now = inner_next
    return solution_field


def solution(mesh):
    in_specs = (
        P("gz", "gy", "gx"),
        P("gz", "gy", "gx"),
        P(),
        P(),
        P(None, "gz", "gy", "gx"),
        P("gz", "gy", "gx"),
        P(),
    )
    out_specs = P("gz", "gy", "gx")
    return jax.shard_map(
        on_device, mesh=mesh, in_specs=in_specs, out_specs=out_specs, check_vma=False
    )
```

profile of v0, /device:TPU:1, one launch (start us, length us, event | category | flops | bytes accessed | tf_op | source)
XLA Modules:
  0.0 952.4 jit_solution(13067103592180606793)
XLA Ops:
  1.0 4.0 collective-permute-start
  6.4 3.3 collective-permute-done.1
  9.9 3.5 collective-permute-start.2
  14.9 3.3 collective-permute-done.3
  18.2 5.9 collective-permute-start.5
  27.6 3.2 collective-permute-start.6
  32.1 3.9 collective-permute-done.7
  36.1 3.5 collective-permute-start.8
  41.0 4.4 collective-permute-done.9
  45.5 6.3 collective-permute-start.10
  57.0 2.9 collective-permute-start.12
  61.3 3.3 collective-permute-done.13
  64.7 4.8 collective-permute-start.14
  71.0 106.3 %psum.64 = f32[256]{0:T(256)S(1)} all-reduce(f32[256]{0:T(256)S(1)} %mul.452), channel_id=1, replica_groups=mesh['gx'=4,'gy'=16,'gz'=8] {'gx','gy','gz'}, use_global_device_ids=true, to_apply=%region_4.5 | all-reduce | flops 256 | bytes 2048 | tf_op jit(solution)/shard_map/psum | solution.py:65
  198.0 4.8 collective-permute-start.22
  208.7 3.1 collective-permute-start.24
  213.1 3.5 collective-permute-done.25
  220.5 3.4 collective-permute-done.27
  224.0 4.4 collective-permute-start.28
  230.3 3.1 collective-permute-done.29
  234.2 102.4 %all-reduce.2 = (f32[]{:T(128)}, f32[]{:T(128)}) all-reduce(f32[]{:T(128)} %get-tuple-element.31, f32[]{:T(128)} %get-tuple-element.29), channel_id=1, replica_groups=mesh['gx'=4,'gy'=16,'gz'=8] {'gx','gy','gz'}, use_global_device_ids=true, to_apply=%region_3.4 | all-reduce | flops 2 | bytes 16 | tf_op jit(solution)/shard_map/psum | solution.py:68
  342.5 3.3 collective-permute-done.31
  348.6 3.1 collective-permute-done.33
  351.7 4.6 collective-permute-start.34
  358.3 3.1 collective-permute-done.35
  361.7 3.6 collective-permute-start.36
  366.6 3.3 collective-permute-done.37
  370.1 2.8 collective-permute-start.38
  374.2 3.6 collective-permute-done.39
  377.9 4.3 collective-permute-start.40
  384.1 3.1 collective-permute-done.41
  391.4 3.3 collective-permute-done.43
  394.9 4.8 collective-permute-start.44
  401.4 3.2 collective-permute-done.45
  404.7 4.3 collective-permute-start.46
  411.1 3.0 collective-permute-done.47
  414.8 99.8 %all-reduce.1 = (f32[256]{0:T(256)S(1)}, f32[]{:T(128)}) all-reduce(f32[256]{0:T(256)S(1)} %mul.492, f32[]{:T(128)} %get-tuple-element.23), channel_id=1, replica_groups=mesh['gx'=4,'gy'=16,'gz'=8] {'gx','gy','gz'}, use_global_device_ids=true, to_apply=%region_10.11 | all-reduce | flops 257 | bytes 2056 | tf_op jit(solution)/shard_map/psum | solution.py:65
  520.8 3.3 collective-permute-done.49
  527.7 3.1 collective-permute-done.51
  530.8 5.2 collective-permute-start.52
  537.9 3.1 collective-permute-done.53
  541.8 102.4 %psum.68 = f32[]{:T(128)} all-reduce(f32[]{:T(128)} %get-tuple-element.19), channel_id=1, replica_groups=mesh['gx'=4,'gy'=16,'gz'=8] {'gx','gy','gz'}, use_global_device_ids=true, to_apply=%region_13.14 | all-reduce | flops 1 | bytes 8 | tf_op jit(solution)/shard_map/psum | solution.py:108
  647.9 3.3 collective-permute-done.55
  654.1 3.1 collective-permute-done.57
  657.3 5.4 collective-permute-start.58
  664.6 3.1 collective-permute-done.59
  668.0 2.8 collective-permute-start.60
  672.2 3.6 collective-permute-done.61
  675.9 3.1 collective-permute-start.62
  680.3 3.3 collective-permute-done.63
  683.7 4.3 collective-permute-start.64
  689.9 3.1 collective-permute-done.65
  693.3 3.6 collective-permute-start.66
  698.3 3.3 collective-permute-done.67
  701.7 4.8 collective-permute-start.68
  708.3 3.2 collective-permute-done.69
  711.5 4.3 collective-permute-start.70
  717.9 3.0 collective-permute-done.71
  721.7 99.8 %all-reduce = (f32[256]{0:T(256)S(1)}, f32[]{:T(128)}) all-reduce(f32[256]{0:T(256)S(1)} %mul.534, f32[]{:T(128)} %get-tuple-element.15), channel_id=1, replica_groups=mesh['gx'=4,'gy'=16,'gz'=8] {'gx','gy','gz'}, use_global_device_ids=true, to_apply=%region_16.17 | all-reduce | flops 257 | bytes 2056 | tf_op jit(solution)/shard_map/psum | solution.py:65
  827.6 3.3 collective-permute-done.73
  834.5 3.1 collective-permute-done.75
  837.7 5.2 collective-permute-start.76
  844.8 3.1 collective-permute-done.77
  848.7 102.4 %psum.71 = f32[]{:T(128)} all-reduce(f32[]{:T(128)} %fusion.25), channel_id=1, replica_groups=mesh['gx'=4,'gy'=16,'gz'=8] {'gx','gy','gz'}, use_global_device_ids=true, to_apply=%region_19.20 | all-reduce | flops 1 | bytes 8 | tf_op jit(solution)/shard_map/psum | solution.py:108
  (193 shorter events, 116.5 us)
Async XLA Ops:
  1.0 5.3 collective-permute-start
  5.1 4.7 collective-permute-start.1
  9.9 5.0 collective-permute-start.2
  13.4 4.7 collective-permute-start.3
  18.2 8.3 collective-permute-start.5
  27.6 4.5 collective-permute-start.6
  30.8 5.2 collective-permute-start.7
  36.1 4.9 collective-permute-start.8
  39.7 5.7 collective-permute-start.9
  45.5 9.3 collective-permute-start.10
  51.7 5.1 collective-permute-start.11
  57.0 4.2 collective-permute-start.12
  60.0 4.7 collective-permute-start.13
  64.7 112.6 %collective-permute-start.14 = (f32[8,1,130]{2,1,0:T(1,128)S(1)}, f32[8,1,130]{2,1,0:T(1,128)S(1)}, u32[]{:S(2)}, u32[]{:S(2)}) collective-permute-start(f32[8,1,130]{2,1,0:T(1,128)S(1)} %get-tuple-element.86), channel_id=1, source_target_pairs={{0,8},{8,16},{16,24},{24,32},{32,40},{40,48},{48,56},{56,64},{64,7... | collective-permute-start | bytes 12488 | tf_op jit(solution)/shard_map/ppermute | solution.py:20
  69.6 107.8 %collective-permute-start.15 = (f32[8,1,130]{2,1,0:T(1,128)S(1)}, f32[8,1,130]{2,1,0:T(1,128)S(1)}, u32[]{:S(2)}, u32[]{:S(2)}) collective-permute-start(f32[8,1,130]{2,1,0:T(1,128)S(1)} %get-tuple-element.87), channel_id=1, source_target_pairs={{8,0},{16,8},{24,16},{32,24},{40,32},{48,40},{56,48},{64,56},{72,6... | collective-permute-start | bytes 12488 | tf_op jit(solution)/shard_map/ppermute | solution.py:21
  177.5 4.6 collective-permute-start.16
  179.4 5.1 collective-permute-start.17
  184.7 4.4 collective-permute-start.18
  187.1 4.7 collective-permute-start.19
  193.5 4.4 collective-permute-start.21
  198.0 7.1 collective-permute-start.22
  202.8 5.1 collective-permute-start.23
  208.7 4.4 collective-permute-start.24
  211.8 4.9 collective-permute-start.25
  219.2 4.7 collective-permute-start.27
  224.0 6.3 collective-permute-start.28
  228.4 5.1 collective-permute-start.29
  341.2 4.7 collective-permute-start.31
  347.3 4.4 collective-permute-start.33
  351.7 6.6 collective-permute-start.34
  356.4 5.1 collective-permute-start.35
  361.7 4.9 collective-permute-start.36
  365.3 4.7 collective-permute-start.37
  372.9 4.9 collective-permute-start.39
  377.9 6.2 collective-permute-start.40
  382.2 5.1 collective-permute-start.41
  390.1 4.7 collective-permute-start.43
  394.9 6.6 collective-permute-start.44
  399.7 4.9 collective-permute-start.45
  404.7 6.4 collective-permute-start.46
  409.0 5.1 collective-permute-start.47
  519.5 4.7 collective-permute-start.49
  526.4 4.4 collective-permute-start.51
  530.8 7.1 collective-permute-start.52
  536.0 5.1 collective-permute-start.53
  646.5 4.7 collective-permute-start.55
  652.8 4.4 collective-permute-start.57
  657.3 7.4 collective-permute-start.58
  662.7 5.1 collective-permute-start.59
  670.9 4.9 collective-permute-start.61
  675.9 4.4 collective-permute-start.62
  679.0 4.6 collective-permute-start.63
  683.7 6.2 collective-permute-start.64
  688.0 5.1 collective-permute-start.65
  693.3 4.9 collective-permute-start.66
  696.9 4.7 collective-permute-start.67
  701.7 6.6 collective-permute-start.68
  706.5 4.9 collective-permute-start.69
  711.5 6.4 collective-permute-start.70
  715.8 5.1 collective-permute-start.71
  826.3 4.7 collective-permute-start.73
  833.2 4.4 collective-permute-start.75
  837.7 7.1 collective-permute-start.76
  842.9 5.1 collective-permute-start.77
  (17 other events, 284.1 us)
where the time goes:
time: 956 us; the launch traced here: 952 us
  blocking collectives  613 us (64%)
  starting transfers between devices  195 us (20%)
  waiting for transfers between devices  119 us (12%)
  other arithmetic  12.1 us (1%)
    psum x3, blocking collectives, precondition(): coarse = lax.psum(local_coarse, ('gx', 'gy', 'gz'))  306 us
    psum x2, blocking collectives, on_device(): lax.psum(jnp.sum(direction * image), ('gx', 'gy', 'gz'))  205 us
    ppermute x39, starting transfers between devices, with_halo(): before = lax.ppermute(last, axis, up)  132 us
    ppermute x39, waiting for transfers between devices, with_halo(): after = lax.ppermute(first, axis, down)  118 us
    psum x1, blocking collectives, precondition(): inner_part = lax.psum(local_inner, ('gx', 'gy', 'gz'))  102 us
    ppermute x39, starting transfers between devices, with_halo(): after = lax.ppermute(first, axis, down)  63.2 us
  transfers between devices with their start and end apart: 78, of which 38 were waited for; matrix products, arithmetic and copies ran while one was open for 0% of the time, Pallas kernels for 0%

commit v1 on v0

v1 whole, which is shorter than its diff:
```python
import functools

import jax
import jax.numpy as jnp
from jax import lax
from jax.experimental import pallas as pl
from jax.experimental.pallas import tpu as pltpu
from jax.sharding import PartitionSpec as P

RELAX = 0.6
BASIS = 32
OWNERS = 8
F32 = jnp.float32
PLANE = ("gx", "gz")
VM = pl.BlockSpec(memory_space=pltpu.VMEM)
SM = pl.BlockSpec(memory_space=pltpu.SMEM)


def call(body, outs, ins, scratch=(), smem=()):
    single = isinstance(outs[0], int)
    shapes = [outs] if single else outs
    shapes = [jax.ShapeDtypeStruct(s, F32) for s in shapes]
    specs = [SM if i in smem else VM for i in range(len(ins))]
    res = pl.pallas_call(
        body, out_shape=shapes, in_specs=specs, out_specs=[VM] * len(shapes),
        scratch_shapes=[pltpu.VMEM(s, d) for s, d in scratch],
        compiler_params=pltpu.CompilerParams(vmem_limit_bytes=40 * 2**20),
    )(*ins)
    return res[0] if single else res


def iota(shape, dim):
    return lax.broadcasted_iota(jnp.int32, shape, dim)


def spread(row, rows):
    return jnp.broadcast_to(row, (rows, row.shape[1]))


def harmonic(a, b):
    total = a + b
    return 2.0 * a * b / jnp.where(total > 0, total, 1.0)


def fit(v, lane):
    return jnp.sum(jnp.where(lane, v, 0.0), axis=1, keepdims=True)


def total(v):
    return jnp.sum(jnp.sum(v, axis=0, keepdims=True), axis=1, keepdims=True)


def near_column(vrow, owner):
    k, j = iota((BASIS, 256), 0), iota((BASIS, 256), 1)
    want = spread(owner.astype(jnp.int32), BASIS) * BASIS + k
    return fit(spread(vrow, BASIS), j == want)


def solve(c_inv, crow):
    n = c_inv.shape[0]
    col = jnp.sum(c_inv[...] * spread(crow, n), axis=1, keepdims=True)
    return jnp.sum(jnp.where(iota((n, n), 0) == iota((n, n), 1), col, 0.0), axis=0, keepdims=True)


def times_e(e_ref, vrow):
    acc = jnp.zeros((OWNERS, 256), F32)
    o, j = iota((OWNERS, 256), 0), iota((OWNERS, 256), 1)
    for m in range(BASIS):
        col = fit(spread(vrow, OWNERS), j == o * BASIS + m)
        acc = acc + col * jnp.concatenate([e_ref[m, 0], e_ref[m, 1]], axis=1)
    return jnp.sum(acc, axis=0, keepdims=True)


def project(bt_ref, tiles):
    acc = jnp.zeros((BASIS, 128), F32)
    for z in range(8):
        for y in range(8):
            acc = acc + bt_ref[z * 8 + y] * spread(tiles[z][y:y + 1, :], BASIS)
    col = jnp.sum(acc, axis=1, keepdims=True)
    k, lane = iota((BASIS, 128), 0), iota((BASIS, 128), 1)
    return jnp.sum(jnp.where(lane % BASIS == k, col, 0.0), axis=0, keepdims=True)


def brick_value(bt_ref, col):
    c = jnp.broadcast_to(col, (BASIS, 128))
    return [jnp.sum(bt_ref[z * 8:z * 8 + 8] * c[None], axis=1) for z in range(8)]


def face_value(f_ref, col):
    return jnp.sum(f_ref[...] * jnp.broadcast_to(col, (BASIS, 128))[None], axis=1)


def line_value(fx, col):
    return jnp.sum(fx * jnp.broadcast_to(col, (BASIS, 128)), axis=0, keepdims=True)


def prolong(bt_ref, faces, own_rows, vrow):
    fxl, fxr, fym, fyp, fzm, fzp = faces
    cols = [near_column(vrow, o) for o in own_rows]
    mine = brick_value(bt_ref, cols[0])
    left = spread(line_value(fxl[...], cols[1]), 8)
    right = spread(line_value(fxr[...], cols[2]), 8)
    ym, yp = face_value(fym, cols[3]), face_value(fyp, cols[4])
    zm, zp = face_value(fzm, cols[5]), face_value(fzp, cols[6])
    sub, lane = iota((8, 128), 0), iota((8, 128), 1)
    zero = jnp.zeros((8, 128), F32)
    planes = {}
    for z in range(8):
        r = fit(right, lane == z * 8 + sub)
        l = fit(left, lane == 64 + z * 8 + sub)
        side = jnp.where(lane == 0, r, jnp.where(lane == 127, l, 0.0))
        beyond = jnp.where(sub == 0, spread(yp[z:z + 1, :], 8),
                           jnp.where(sub == 7, spread(ym[z:z + 1, :], 8), 0.0))
        planes[z] = jnp.concatenate([
            jnp.concatenate([mine[z], side], axis=1),
            jnp.concatenate([beyond, zero], axis=1)], axis=0)
    for z, t in ((8, zp), (-1, zm)):
        planes[z] = jnp.concatenate([
            jnp.concatenate([t, zero], axis=1),
            jnp.zeros((8, 256), F32)], axis=0)
    return planes


def around(c_ref, s, z):
    p = z % 16
    v = s[z]
    return (
        c_ref[0, p] * pltpu.roll(v, 255, 1) + c_ref[1, p] * pltpu.roll(v, 1, 1)
        + c_ref[2, p] * pltpu.roll(v, 15, 0) + c_ref[3, p] * pltpu.roll(v, 1, 0)
        + c_ref[4, p] * s[z + 1] + c_ref[5, p] * s[z - 1])


def smooth(c_ref, r):
    s = {z: r[z] * c_ref[6, z % 16] for z in range(-4, 12)}
    q = {z: RELAX * s[z] for z in range(-3, 11)}
    for lo, hi in ((-3, 11), (-2, 10), (-1, 9)):
        s = {z: (1 - RELAX) * s[z] + q[z] + around(c_ref, s, z) for z in range(lo, hi)}
    return s


def operate(c_ref, d_ref, s):
    return [
        d_ref[z] * (s[z] - (1 / RELAX) * around(c_ref, s, z))[:8, :128] for z in range(8)]


def plane_of(own_ref, up_ref, down_ref, z, *lead):
    if z < 0:
        ref, i = down_ref, z + 4
    elif z >= 8:
        ref, i = up_ref, z - 8
    else:
        ref, i = own_ref, z
    t = [[ref[lead + (x, i, y)] for x in range(2)] for y in range(2)]
    return jnp.concatenate([jnp.concatenate(t[0], axis=1), jnp.concatenate(t[1], axis=1)], axis=0)


def first_body(perm_ref, store_ref, b_ref, cls_ref, basis_ref, f_ref, bt_ref, fx_ref):
    ks, sts = [], []
    for z in range(8):
        c = cls_ref[z]
        k = jnp.zeros((8, 128), F32)
        st = jnp.zeros((8, 128), F32)
        for i in range(16):
            k = jnp.where(c == i, perm_ref[i], k)
            st = jnp.where(c == i, store_ref[i], st)
        ks.append(k)
        sts.append(st)
    sub = iota((8, 128), 0)
    tz = harmonic(ks[3], ks[4])
    for z in range(8):
        f_ref[0, z] = b_ref[z]
        f_ref[1, z] = ks[z]
        f_ref[2, z] = sts[z]
        up = harmonic(ks[z], pltpu.roll(ks[z], 7, 0))
        down = pltpu.roll(up, 1, 0)
        f_ref[3, z] = sts[z] + jnp.where(sub == 3, up, jnp.where(sub == 4, down, 0.0))
        f_ref[4, z] = sts[z] + tz if z in (3, 4) else sts[z]
    lane = iota((BASIS, 128), 1)
    lo = jnp.zeros((BASIS, 128), F32)
    hi = jnp.zeros((BASIS, 128), F32)
    for z in range(8):
        t = jnp.swapaxes(basis_ref[:, z].astype(F32), 0, 1)
        bt_ref[z * 8:z * 8 + 8] = t
        for y in range(8):
            i = z * 8 + y
            r = pltpu.roll(t[y], i, 1) if i else t[y]
            lo = jnp.where(lane == i, r, lo)
            hi = jnp.where(lane == (i - 1) % 128, r, hi)
    fx_ref[...] = jnp.where(lane < 64, lo, pltpu.roll(hi, 65, 1))


def setup_body(own_ref, up_ref, down_ref, owners_ref, bt_ref, fx_ref, fxl_ref, fxr_ref, fym_ref,
               fyp_ref, fzm_ref, fzp_ref, c_ref, d_ref, s_ref, b4_ref, msg_ref, k_ref, t_ref,
               bf_ref, wh_ref, wl_ref):
    lane = iota((16, 256), 1)
    sub = iota((16, 256), 0)
    for z in range(-4, 12):
        k_ref[z % 16] = plane_of(own_ref, up_ref, down_ref, z, 1)
        b4_ref[z % 16] = plane_of(own_ref, up_ref, down_ref, z, 0)
    for z in range(-4, 12):
        p = z % 16
        k = k_ref[p]
        t_ref[0, p] = jnp.where(lane == 191, 0.0, harmonic(k, pltpu.roll(k, 255, 1)))
        t_ref[1, p] = jnp.where(sub == 11, 0.0, harmonic(k, pltpu.roll(k, 15, 0)))
        if z < 11:
            t_ref[2, p] = harmonic(k, k_ref[(z + 1) % 16])
        else:
            t_ref[2, p] = jnp.zeros((16, 256), F32)
    for z in range(-4, 12):
        p = z % 16
        tx, ty, tz = t_ref[0, p], t_ref[1, p], t_ref[2, p]
        xm, ym, zm = pltpu.roll(tx, 1, 1), pltpu.roll(ty, 1, 0), t_ref[2, (z - 1) % 16]
        st = plane_of(own_ref, up_ref, down_ref, z, 2)
        diag = st + (tx + xm) + (ty + ym) + (tz + zm)
        inv = jnp.where(diag > 0, 1.0 / jnp.where(diag > 0, diag, 1.0), 0.0)
        ri = RELAX * inv
        for i, t in enumerate((tx, xm, ty, ym, tz, zm)):
            c_ref[i, p] = ri * t
        c_ref[6, p] = inv
        if 0 <= z < 8:
            d_ref[z] = diag[:8, :128]
    s = smooth(c_ref, {z: b4_ref[z % 16] for z in range(-4, 12)})
    for z in range(-1, 9):
        s_ref[z + 1] = s[z]
    a = operate(c_ref, d_ref, s)
    bs = jnp.zeros((8, 128), F32)
    sas = jnp.zeros((8, 128), F32)
    rough = []
    for z in range(8):
        so = s[z][:8, :128]
        b = b4_ref[z][:8, :128]
        rough.append(b.astype(jnp.bfloat16).astype(F32))
        bs = bs + b * so
        sas = sas + a[z] * so
    crow = project(bt_ref, rough)
    grow = project(bt_ref, a)
    ln = iota((1, 128), 1)
    row = lambda ref_t, y: spread(ref_t[y:y + 1, :128], BASIS)
    for z in range(8):
        tx, ty, tz = t_ref[0, z], t_ref[1, z], t_ref[2, z]
        zmn = t_ref[2, (z - 1) % 16]
        txm = pltpu.roll(tx, 1, 1)
        tym = pltpu.roll(ty, 1, 0)
        txi = jnp.where(lane == 127, 0.0, tx)
        txmi = jnp.where(lane == 0, 0.0, txm)
        dz = d_ref[z]
        for y in range(8):
            i = z * 8 + y
            v = bt_ref[i]
            w = row(dz, y) * v - row(txi, y) * pltpu.roll(v, 127, 1) - row(txmi, y) * pltpu.roll(v, 1, 1)
            if y < 7:
                w = w - row(ty, y) * bt_ref[i + 1]
            if y > 0:
                w = w - row(tym, y) * bt_ref[i - 1]
            if z < 7:
                w = w - row(tz, y) * bt_ref[i + 8]
            if z > 0:
                w = w - row(zmn, y) * bt_ref[i - 8]
            high = w.astype(jnp.bfloat16)
            at = slice(i * 128, i * 128 + 128)
            bf_ref[:, at] = v.astype(jnp.bfloat16)
            wh_ref[:, at] = high
            wl_ref[:, at] = (w - high.astype(F32)).astype(jnp.bfloat16)
    nt = (((1,), (1,)), ((), ()))
    dot = lambda l, r: lax.dot_general(l, r, nt, preferred_element_type=F32)
    blocks = [dot(bf_ref[...], wh_ref[...]) + dot(bf_ref[...], wl_ref[...])]

    def face(mine, trans, theirs):
        w = theirs * trans
        high = w.astype(jnp.bfloat16)
        m = mine.astype(jnp.bfloat16)
        return dot(m, high) + dot(m, (w - high.astype(F32)).astype(jnp.bfloat16))

    s8, l8 = iota((8, 128), 0), iota((8, 128), 1)

    def line(pick):
        acc = jnp.zeros((8, 128), F32)
        for z in range(8):
            acc = acc + jnp.where(l8 == z * 8 + s8, pick(z), 0.0)
        return spread(jnp.sum(acc, axis=0, keepdims=True), BASIS)

    txl = line(lambda z: t_ref[0, z][:8, 255:256])
    txr = line(lambda z: t_ref[0, z][:8, 127:128])
    fx = fx_ref[...]
    blocks.append(-face(fx, txl, pltpu.roll(fxl_ref[...], 64, 1)))
    blocks.append(-face(pltpu.roll(fx, 64, 1), txr, fxr_ref[...]))
    acc = jnp.zeros((4, BASIS, BASIS), F32)
    accs = [acc[0], acc[1], acc[2], acc[3]]
    for z in range(8):
        accs[0] = accs[0] - face(bt_ref[z * 8], spread(t_ref[1, z][15:16, :128], BASIS), fym_ref[z])
        accs[1] = accs[1] - face(bt_ref[z * 8 + 7], spread(t_ref[1, z][7:8, :128], BASIS), fyp_ref[z])
    for y in range(8):
        accs[2] = accs[2] - face(bt_ref[y], spread(t_ref[2, 15][y:y + 1, :128], BASIS), fzm_ref[y])
        accs[3] = accs[3] - face(bt_ref[56 + y], spread(t_ref[2, 7][y:y + 1, :128], BASIS), fzp_ref[y])
    blocks += accs
    elo = jnp.zeros((BASIS, 128), F32)
    ehi = jnp.zeros((BASIS, 128), F32)
    group = iota((BASIS, 128), 1) // BASIS
    for n in range(7):
        tiled = jnp.concatenate([blocks[n]] * 4, axis=1)
        o = spread(owners_ref[n:n + 1, :], BASIS).astype(jnp.int32)
        elo = elo + jnp.where(group == o, tiled, 0.0)
        ehi = ehi + jnp.where(group + 4 == o, tiled, 0.0)
    common = jnp.where(s8 == 2, spread(crow, 8), 0.0) + jnp.where(s8 == 3, spread(grow, 8), 0.0)
    common = common + jnp.where(s8 == 4, spread(jnp.sum(bs, axis=0, keepdims=True), 8), 0.0)
    common = common + jnp.where(s8 == 5, spread(jnp.sum(sas, axis=0, keepdims=True), 8), 0.0)
    common = common + jnp.where(s8 == 6, spread(owners_ref[0:1, :], 8), 0.0)
    for m in range(BASIS):
        msg_ref[m] = common + jnp.where(s8 == 0, spread(elo[m:m + 1, :], 8), 0.0) + jnp.where(
            s8 == 1, spread(ehi[m:m + 1, :], 8), 0.0)


def place(t, owner):
    group = iota((8, 128), 1) // BASIS
    o = spread(owner, 8).astype(jnp.int32)
    return jnp.where(group == o, t, 0.0), jnp.where(group + 4 == o, t, 0.0)


def gather_body(got_ref, msg_ref, own_ref):
    zero = jnp.zeros((8, 128), F32)
    elo, ehi, clo, chi, plain = zero, zero, zero, zero, zero
    sub = iota((8, 128), 0)
    for m in range(got_ref.shape[0]):
        t = got_ref[m]
        owner = t[6:7, :]
        hit = sub == spread(owner, 8).astype(jnp.int32)
        elo = elo + jnp.where(hit, spread(t[0:1, :], 8), 0.0)
        ehi = ehi + jnp.where(hit, spread(t[1:2, :], 8), 0.0)
        a, b = place(t, owner)
        clo, chi, plain = clo + a, chi + b, plain + t
        own_ref[m:m + 1, :] = owner
    row = lambda t, i: spread(t[i:i + 1, :], 8)
    rows = [row(clo, 2), row(chi, 2), row(clo, 3), row(chi, 3), row(plain, 4), row(plain, 5)]
    out = zero
    for i, r in enumerate(rows):
        out = jnp.where(sub == i, r, out)
    for n in range(msg_ref.shape[0]):
        msg_ref[n, 0] = elo
        msg_ref[n, 1] = ehi
        msg_ref[n, 2] = out


def wide(t, i):
    return jnp.concatenate([t[i:i + 1, :], t[i + 1:i + 2, :]], axis=1)


def owner_rows(owners_ref):
    return [jnp.concatenate([owners_ref[n:n + 1, :]] * 2, axis=1) for n in range(7)]


def begin_body(got_ref, cinv_ref, owners_ref, bt_ref, fxl, fxr, fym, fyp, fzm, fzp, c_ref, d_ref,
               s_ref, z_ref, w_ref, msg_ref, state_ref):
    e0 = got_ref[0, 0]
    e1 = got_ref[0, 1]
    t = got_ref[0, 2]
    for n in range(1, got_ref.shape[0]):
        e0, e1, t = e0 + got_ref[n, 0], e1 + got_ref[n, 1], t + got_ref[n, 2]
    crow = wide(t, 0)
    vrow = solve(cinv_ref, crow)
    state_ref[0] = t
    state_ref[1] = spread(vrow[:, :128], 8)
    state_ref[2] = spread(vrow[:, 128:], 8)
    z = prolong(bt_ref, (fxl, fxr, fym, fyp, fzm, fzp), owner_rows(owners_ref), vrow)
    z = {i: z[i] + s_ref[i + 1] for i in range(-1, 9)}
    w = operate(c_ref, d_ref, z)
    lane = iota((8, 128), 1)
    ride = jnp.zeros((8, 128), F32)
    for i in range(8):
        z_ref[i] = z[i][:8, :128]
        w_ref[i] = w[i]
        ride = jnp.where(lane // 8 == i, pltpu.roll(w[i], 4 + 8 * i, 1), ride)
    for m in range(msg_ref.shape[0]):
        msg_ref[m, 0] = e0
        msg_ref[m, 1] = e1
        msg_ref[m, 2] = ride


def ride_body(at_ref, got_ref, w_ref, out_ref):
    left = jnp.where(at_ref[0] > 0, got_ref[jnp.maximum(at_ref[1], 0), 2], 0.0)
    right = jnp.where(at_ref[0] < at_ref[3] - 1, got_ref[jnp.minimum(at_ref[2], BASIS - 1), 2], 0.0)
    lane = iota((8, 128), 1)
    for z in range(8):
        l = pltpu.roll(left, (124 - 8 * z) % 128, 1)
        r = pltpu.roll(right, (124 - 8 * z) % 128, 1)
        out_ref[0, z] = w_ref[z]
        out_ref[1, z] = jnp.where(lane < 4, r, jnp.where(lane >= 124, l, 0.0))


def next_body(state_ref, e_ref, cinv_ref, owners_ref, bt_ref, fxl, fxr, fym, fyp, fzm, fzp, c_ref,
              d_ref, s_ref, b4_ref, own_ref, up_ref, down_ref, z_ref, r_ref, out_ref):
    t = state_ref[0]
    vrow = jnp.concatenate([state_ref[1][0:1, :], state_ref[2][0:1, :]], axis=1)
    crow, grow = wide(t, 0), wide(t, 2)
    ev = times_e(e_ref, vrow)
    lanes = lambda v: jnp.sum(v, axis=1, keepdims=True)
    inner = lanes(t[4:5, :]) + lanes(crow * vrow)
    curve = lanes(t[5:6, :]) + lanes((2.0 * grow + ev) * vrow)
    step = inner / curve
    c1 = crow - step * (grow + ev)
    v1 = solve(cinv_ref, c1)
    r1 = {z: b4_ref[z % 16] - step * plane_of(own_ref, up_ref, down_ref, z) for z in range(-4, 12)}
    s1 = smooth(c_ref, r1)
    z1 = prolong(bt_ref, (fxl, fxr, fym, fyp, fzm, fzp), owner_rows(owners_ref), v1)
    z1 = {z: z1[z] + s1[z] for z in range(-1, 9)}
    w1 = operate(c_ref, d_ref, z1)
    zero = jnp.zeros((8, 128), F32)
    sums = [zero, zero, zero, zero]
    for z in range(8):
        r1o = r1[z][:8, :128]
        r2 = r1o - step * w1[z]
        s0o, s1o = s_ref[z + 1][:8, :128], s1[z][:8, :128]
        z_ref[z] = z1[z][:8, :128]
        r_ref[z] = r2
        for i, (a, b) in enumerate(((r1o, s0o), (r1o, s1o), (r2, s0o), (r2, s1o))):
            sums[i] = sums[i] + a * b
    sub, lane = iota((8, 128), 0), iota((8, 128), 1)
    tile = zero
    for i in range(4):
        tile = jnp.where(lane == i, total(sums[i]), tile)
    out_ref[0] = tile
    wide_rows = [c1[:, :128], c1[:, 128:], v1[:, :128], v1[:, 128:]]
    tile = zero
    for i, r in enumerate(wide_rows):
        tile = jnp.where(sub == i, spread(r, 8), tile)
    tile = jnp.where(sub == 4, step, jnp.where(sub == 5, curve, tile))
    out_ref[1] = tile


def last_body(part_ref, owners_ref, bt_ref, c_ref, d_ref, own_ref, up_ref, down_ref, s_ref, msg_ref):
    r2 = {z: plane_of(own_ref, up_ref, down_ref, z) for z in range(-4, 12)}
    s2 = smooth(c_ref, r2)
    a = operate(c_ref, d_ref, s2)
    rs = jnp.zeros((8, 128), F32)
    sas = jnp.zeros((8, 128), F32)
    ro = []
    for z in range(8):
        so = s2[z][:8, :128]
        s_ref[z] = so
        ro.append(r2[z][:8, :128])
        rs = rs + ro[z] * so
        sas = sas + a[z] * so
    crow = project(bt_ref, ro)
    hrow = project(bt_ref, a)
    lane, sub = iota((8, 128), 1), iota((8, 128), 0)
    scal = jnp.where(lane == 4, total(rs), jnp.where(lane == 5, total(sas), part_ref[0]))
    tile = jnp.where(sub == 2, spread(crow, 8), jnp.where(sub == 3, spread(hrow, 8), jnp.where(
        sub == 4, scal, jnp.where(sub == 6, spread(owners_ref[0:1, :], 8), 0.0))))
    for m in range(msg_ref.shape[0]):
        msg_ref[m] = tile


def gather_last_body(got_ref, msg_ref):
    zero = jnp.zeros((8, 128), F32)
    clo, chi, plain = zero, zero, zero
    sub = iota((8, 128), 0)
    for m in range(got_ref.shape[0]):
        t = got_ref[m]
        a, b = place(t, t[6:7, :])
        clo, chi, plain = clo + a, chi + b, plain + t
    row = lambda t, i: spread(t[i:i + 1, :], 8)
    rows = [row(clo, 2), row(chi, 2), row(clo, 3), row(chi, 3), row(plain, 4)]
    out = zero
    for i, r in enumerate(rows):
        out = jnp.where(sub == i, r, out)
    for n in range(msg_ref.shape[0]):
        msg_ref[n] = out


def finish_body(got_ref, state_ref, out1_ref, e_ref, cinv_ref, owners_ref, bt_ref, z0_ref, z1_ref,
                s2_ref, x_ref):
    t = got_ref[0]
    for n in range(1, got_ref.shape[0]):
        t = t + got_ref[n]
    c2, h2 = wide(t, 0), wide(t, 2)
    v0 = jnp.concatenate([state_ref[1][0:1, :], state_ref[2][0:1, :]], axis=1)
    o1 = out1_ref[1]
    c1, v1 = wide(o1, 0), wide(o1, 2)
    step, curve = o1[4:5, 0:1], o1[5:6, 0:1]
    v2 = solve(cinv_ref, c2)
    ev2 = times_e(e_ref, v2)
    lanes = lambda v: jnp.sum(v, axis=1, keepdims=True)
    sums = [t[4:5, i:i + 1] for i in range(6)]
    m10 = sums[0] + lanes(c1 * v0)
    m11 = sums[1] + lanes(c1 * v1)
    m20 = sums[2] + lanes(c2 * v0)
    m21 = sums[3] + lanes(c2 * v1)
    m22 = sums[4] + lanes(c2 * v2)
    g00 = curve
    g01 = (m10 - m11) / step
    g02 = (m20 - m21) / step
    g11 = (m11 - m21) / step
    g12 = (m21 - m22) / step
    g22 = sums[5] + lanes((2.0 * h2 + ev2) * v2)
    l1 = g01 / g00
    l2 = g02 / g00
    d11 = g11 - l1 * g01
    d12 = g12 - l1 * g02
    d22 = g22 - l2 * g02
    f1 = m11 - l1 * m10
    f2 = m21 - l2 * m10
    k2 = d12 / d11
    y2 = (f2 - k2 * f1) / (d22 - k2 * d12)
    y1 = (f1 - d12 * y2) / d11
    y0 = step + (m10 - g01 * y1 - g02 * y2) / g00
    own = jnp.concatenate([owners_ref[0:1, :]] * 2, axis=1)
    bv = brick_value(bt_ref, near_column(v2, own))
    for z in range(8):
        x_ref[z] = y0 * z0_ref[z] + y1 * z1_ref[z] + y2 * (s2_ref[z] + bv[z])


def pair(up_part, down_part, axis):
    size = lax.axis_size(axis)
    up = [(i, i + 1) for i in range(size - 1)]
    down = [(j, i) for i, j in up]
    below = lax.ppermute(up_part, axis, up)
    above = lax.ppermute(down_part, axis, down)
    return below, above


def tiles(a):
    return a.reshape((-1, 8, 128))


def on_device(
    right_side, perm_class, class_perm, class_store, coarse_basis, brick_owner, coarse_inverse
):
    group = lax.axis_size("gx") * lax.axis_size("gz")
    rows = lax.axis_size("gy")
    owner = brick_owner.reshape(()).astype(F32)
    owner_tile = jnp.full((1, 8, 128), owner)
    fields, bt, fx = call(
        first_body, [(5, 8, 8, 128), (64, BASIS, 128), (BASIS, 128)],
        [class_perm, class_store, right_side, perm_class, coarse_basis], smem=(0, 1))
    low = lax.broadcasted_iota(jnp.int32, (8, 128), 1) < 64
    half = lax.broadcasted_iota(jnp.int32, (8, 128), 0) < 4
    msg = jnp.concatenate([tiles(fields[:3]), tiles(fx), owner_tile])
    left, right = pair(msg, msg, "gx")
    beside = jnp.where(low, right[:24], left[:24]).reshape(3, 1, 8, 8, 128)
    fxl, fxr = left[24:28].reshape(BASIS, 128), right[24:28].reshape(BASIS, 128)
    ox = (left[28, :1], right[28, :1])
    bt4 = bt.reshape(8, 8, BASIS, 128)
    y_own = jnp.concatenate([jnp.stack(
        [fields[0], fields[1], fields[3]])[:, None], beside], axis=1)
    flat = tiles(y_own)
    below, above = pair(
        jnp.concatenate([flat, tiles(bt4[:, 7]), owner_tile]),
        jnp.concatenate([flat, tiles(bt4[:, 0]), owner_tile]), "gy")
    n = flat.shape[0]
    beyond = jnp.where(half, above[:n], below[:n]).reshape(3, 2, 8, 1, 8, 128)
    fym, fyp = below[n:n + 32].reshape(8, BASIS, 128), above[n:n + 32].reshape(8, BASIS, 128)
    oy = (below[n + 32, :1], above[n + 32, :1])
    own_z = jnp.concatenate([jnp.stack([fields[0], fields[1], fields[4]])[:, None], beside], axis=1)
    own_z = jnp.concatenate([own_z[:, :, :, None], beyond], axis=3)
    up_msg = jnp.concatenate([tiles(own_z[:, :, 4:]), tiles(bt[56:]), owner_tile])
    down_msg = jnp.concatenate([tiles(own_z[:, :, :4]), tiles(bt[:8]), owner_tile])
    below, above = pair(up_msg, down_msg, "gz")
    own_c = jnp.concatenate([jnp.stack([fields[0], fields[1], fields[2]])[:, None], beside], axis=1)
    own_c = jnp.concatenate([own_c[:, :, :, None], beyond], axis=3)
    n = 3 * 2 * 4 * 2
    z_down, z_up = [a[:n].reshape(3, 2, 4, 2, 8, 128) for a in (below, above)]
    fzm, fzp = [a[n:n + 32].reshape(8, BASIS, 128) for a in (below, above)]
    oz = (below[n + 32, :1], above[n + 32, :1])
    owners = jnp.concatenate([owner_tile[0, :1], *ox, *oy, *oz, owner_tile[0, :1]])
    faces = (fxl, fxr, fym, fyp, fzm, fzp)
    ext = (16, 16, 256)
    brick = (8, 8, 128)
    coef, diag, s0, b4, msg = call(
        setup_body, [(7,) + ext, brick, (10, 16, 256), ext, (group, 8, 128)],
        [own_c, z_up, z_down, owners, bt, fx, *faces],
        scratch=[(ext, F32), ((3,) + ext, F32)] + [((BASIS, 8192), jnp.bfloat16)] * 3)
    got = lax.all_to_all(msg, PLANE, 0, 0)
    msg, _ = call(gather_body, [(rows, 3, 8, 128), (group, 128)], [got])
    got = lax.all_to_all(msg, "gy", 0, 0)
    z0, w0, msg, state = call(
        begin_body, [brick, brick, (group, 3, 8, 128), (3, 8, 128)],
        [got, coarse_inverse, owners, bt, *faces, coef, diag, s0])
    e_all = lax.all_to_all(msg, PLANE, 0, 0)
    gx, gz = lax.axis_index("gx"), lax.axis_index("gz")
    nz = lax.axis_size("gz")
    at = jnp.stack([gx, (gx - 1) * nz + gz, (gx + 1) * nz + gz, jnp.int32(lax.axis_size("gx"))])
    w_x = call(ride_body, (2, 8, 8, 128), [at.astype(jnp.int32), e_all, w0], smem=(0,))

    def rest(f_x):
        below, above = pair(f_x, f_x, "gy")
        own = jnp.stack([f_x, jnp.where(half, above, below)], axis=2)
        below, above = pair(own[:, 4:], own[:, :4], "gz")
        return own, above, below

    z1, r2, out1 = call(
        next_body, [brick, brick, (2, 8, 128)],
        [state, e_all, coarse_inverse, owners, bt, *faces, coef, diag, s0, b4, *rest(w_x)])
    left, right = pair(r2, r2, "gx")
    r_x = jnp.stack([r2, jnp.where(low, right, left)])
    s2, msg = call(
        last_body, [brick, (group, 8, 128)],
        [out1, owners, bt, coef, diag, *rest(r_x)])
    got = lax.all_to_all(msg, PLANE, 0, 0)
    msg = call(gather_last_body, (rows, 8, 128), [got])
    got = lax.all_to_all(msg, "gy", 0, 0)
    return call(
        finish_body, brick,
        [got, state, out1, e_all, coarse_inverse, owners, bt, z0, z1, s2])


def solution(mesh):
    grid = P("gz", "gy", "gx")
    in_specs = (grid, grid, P(), P(), P(None, "gz", "gy", "gx"), grid, P())
    return jax.shard_map(
        on_device, mesh=mesh, in_specs=in_specs, out_specs=grid, check_vma=False)
```

time: 956 us -> 192 us (0.20)
  blocking collectives: 613 us -> 80.3 us
  starting transfers between devices: 195 us -> 61.4 us
  waiting for transfers between devices: 119 us -> 24.5 us
  local copies, waits for them, and re-layouts: 1.94 us -> 12.2 us
    psum x6 -> x0, blocking collectives: 613 us -> none  [the longest x3 306 us: precondition(): coarse = lax.psum(local_coarse, ('gx', 'gy', 'gz'))]
    ppermute x78 -> x16, starting transfers between devices: 195 us -> 54 us  [the longest x8 30.8 us: pair(): below = lax.ppermute(up_part, axis, up)]
    ppermute x78 -> x16, waiting for transfers between devices: 119 us -> 14.9 us  [the longest x8 12.1 us: pair(): below = lax.ppermute(up_part, axis, up)]
    all_to_all x0 -> x4, blocking collectives: none -> 80.3 us  [the longest x2 51.4 us: on_device(): got = lax.all_to_all(msg, 'gy', 0, 0)]
    unnamed x8 -> x74, local copies, waits for them, and re-layouts: 0.48 us -> 12 us
    all_to_all x0 -> x1, waiting for transfers between devices: none -> 9.61 us  [on_device(): e_all = lax.all_to_all(msg, PLANE, 0, 0)]
  transfers between devices with their start and end apart: 78 -> 17, of which waited for: 38 -> 12; matrix products, arithmetic and copies ran while one was open for 0% -> 1% of each run, Pallas kernels for 0% -> 0%
where the time goes in v1:
time: 192 us; the launch traced here: 191 us
  blocking collectives  80.3 us (42%)
  starting transfers between devices  61.4 us (32%)
  waiting for transfers between devices  24.5 us (13%)
  local copies, waits for them, and re-layouts  12.2 us (6%)
  Pallas kernels  8.49 us (4%)
  other arithmetic  2.6 us (1%)
    all_to_all x2, blocking collectives, on_device(): got = lax.all_to_all(msg, 'gy', 0, 0)  51.4 us
    ppermute x8, starting transfers between devices, pair(): below = lax.ppermute(up_part, axis, up)  30.8 us
    all_to_all x2, blocking collectives, on_device(): got = lax.all_to_all(msg, PLANE, 0, 0)  28.8 us
    ppermute x8, starting transfers between devices, pair(): above = lax.ppermute(down_part, axis, down)  23.2 us
    ppermute x8, waiting for transfers between devices, pair(): below = lax.ppermute(up_part, axis, up)  12.1 us
    unnamed x74, local copies, waits for them, and re-layouts  12 us
    all_to_all x1, waiting for transfers between devices, on_device(): e_all = lax.all_to_all(msg, PLANE, 0, 0)  9.61 us
    pallas_call x9, Pallas kernels, call(): pl.pallas_call(body, out_shape=shapes, in_specs=specs, out_specs=[VM] * l...  8.49 us
  transfers between devices with their start and end apart: 17, of which 12 were waited for; matrix products, arithmetic and copies ran while one was open for 1% of the time, Pallas kernels for 0%

profile of v1, /device:TPU:1, one launch (start us, length us, event | category | flops | bytes accessed | tf_op | source)
XLA Modules:
  0.0 190.8 jit_solution(12399982485975169793)
XLA Ops:
  0.0 1.0 copy-done.12
  1.0 0.8 copy-done.26
  1.8 0.8 copy-done.27
  2.6 0.7 copy-done.31
  3.2 0.7 copy-done.32
  3.9 1.1 shard_map.73
  5.6 1.3 collective-permute-start
  6.9 4.7 %collective-permute-start.1 = (f32[29,8,128]{2,1,0:T(8,128)S(1)}, f32[29,8,128]{2,1,0:T(8,128)S(1)}, u32[]{:S(2)}, u32[]{:S(2)}) collective-permute-start(f32[29,8,128]{2,1,0:T(8,128)S(1)} %pad_maximum_fusion.13), channel_id=1, source_target_pairs={{0,128},{128,256},{256,384},{1,129},{129,257},{257,385},{2,130},{1... | collective-permute-start | bytes 356360 | tf_op jit(solution)/shard_map/ppermute | solution.py:515
  11.8 0.1 collective-permute-done
  11.9 1.5 collective-permute-done.1
  13.6 1.3 collective-permute-start.2
  14.9 4.3 %collective-permute-start.3 = (f32[81,8,128]{2,1,0:T(8,128)S(1)}, f32[81,8,128]{2,1,0:T(8,128)S(1)}, u32[]{:S(2)}, u32[]{:S(2)}) collective-permute-start(f32[81,8,128]{2,1,0:T(8,128)S(1)} %get-tuple-element.48), channel_id=1, source_target_pairs={{0,8},{8,16},{16,24},{24,32},{32,40},{40,48},{48,56},{56,64},{64,7... | collective-permute-start | bytes 995336 | tf_op jit(solution)/shard_map/ppermute | solution.py:515
  19.3 2.5 %collective-permute-done.2 = f32[81,8,128]{2,1,0:T(8,128)S(1)} collective-permute-done((f32[81,8,128]{2,1,0:T(8,128)S(1)}, f32[81,8,128]{2,1,0:T(8,128)S(1)}, u32[]{:S(2)}, u32[]{:S(2)}) %collective-permute-start.2) | collective-permute-done | bytes 331808 | tf_op jit(solution)/shard_map/ppermute | solution.py:516
  21.8 1.5 collective-permute-done.3
  23.2 0.1 slice_select_fusion
  23.4 10.0 %collective-permute-start.4 = (f32[81,8,128]{2,1,0:T(8,128)S(1)}, f32[81,8,128]{2,1,0:T(8,128)S(1)}, u32[]{:S(2)}, u32[]{:S(2)}) collective-permute-start(f32[81,8,128]{2,1,0:T(8,128)S(1)} %get-tuple-element.65), channel_id=1, source_target_pairs={{1,0},{2,1},{3,2},{4,3},{5,4},{6,5},{7,6},{9,8},{10,9},{11,10},{12... | collective-permute-start | bytes 995336 | tf_op jit(solution)/shard_map/ppermute | solution.py:516
  33.5 1.9 %collective-permute-start.5 = (f32[81,8,128]{2,1,0:T(8,128)S(1)}, f32[81,8,128]{2,1,0:T(8,128)S(1)}, u32[]{:S(2)}, u32[]{:S(2)}) collective-permute-start(f32[81,8,128]{2,1,0:T(8,128)S(1)} %get-tuple-element.64), channel_id=1, source_target_pairs={{0,1},{1,2},{2,3},{3,4},{4,5},{5,6},{6,7},{8,9},{9,10},{10,11},{11... | collective-permute-start | bytes 995336 | tf_op jit(solution)/shard_map/ppermute | solution.py:515
  35.5 0.8 pad_maximum_fusion.4.own_ref
  36.3 3.1 %collective-permute-done.5 = f32[81,8,128]{2,1,0:T(8,128)S(1)} collective-permute-done((f32[81,8,128]{2,1,0:T(8,128)S(1)}, f32[81,8,128]{2,1,0:T(8,128)S(1)}, u32[]{:S(2)}, u32[]{:S(2)}) %collective-permute-start.5) | collective-permute-done | bytes 331808 | tf_op jit(solution)/shard_map/ppermute | solution.py:515
  39.5 0.0 copy-start
  39.6 1.1 copy-done.9
  40.7 2.4 %shard_map.74 = (f32[7,16,16,256]{3,2,1,0:T(8,128)S(1)}, f32[8,8,128]{2,1,0:T(8,128)S(1)}, f32[10,16,256]{2,1,0:T(8,128)S(1)}, f32[16,16,256]{2,1,0:T(8,128)S(1)}, f32[32,8,128]{2,1,0:T(8,128)S(1)}) custom-call(f32[3,2,8,2,8,128]{5,4,3,2,1,0:T(8,128)S(1)} %copy-done.9, f32[3,2,4,2,8,128]{5,4,3,2,1,0:T(8,128)S(1)} %bitcast.77, ...), custom_call_target="tpu_custom_call" | custom-call | tf_op jit(solution)/shard_map/pallas_call | solution.py:24
  43.1 13.7 %all_to_all.25.got_ref = f32[32,8,128]{2,1,0:T(8,128)S(1)} all-to-all(f32[32,8,128]{2,1,0:T(8,128)S(1)} %get-tuple-element.26), channel_id=1, replica_groups=mesh['gx'=4,'gy'=16,'gz'=8] {'gx','gz'}, dimensions={0} | all-to-all | bytes 262144 | tf_op jit(solution)/shard_map/all_to_all | solution.py:571
  56.7 0.6 shard_map.75
  57.4 29.1 %all_to_all.26.got_ref = f32[16,3,8,128]{3,2,1,0:T(8,128)S(1)} all-to-all(f32[16,3,8,128]{3,2,1,0:T(8,128)S(1)} %get-tuple-element.27), channel_id=1, replica_groups=mesh['gx'=4,'gy'=16,'gz'=8] {'gy'}, dimensions={0} | all-to-all | bytes 393216 | tf_op jit(solution)/shard_map/all_to_all | solution.py:573
  86.5 0.6 shard_map.76
  87.2 0.8 copy-done.13
  87.9 0.6 copy-done.22
  88.5 0.6 copy-done.24
  89.2 0.6 copy-done.28
  89.8 7.3 %all-to-all-start.2 = ((f32[32,3,8,128]{3,2,1,0:T(8,128)}), f32[32,3,8,128]{3,2,1,0:T(8,128)S(1)}, u32[]{:S(2)}, u32[]{:S(2)}) async-start(f32[32,3,8,128]{3,2,1,0:T(8,128)} %copy-done.13), calls=%async_computation.2 | async-start | bytes 786432 | tf_op jit(solution)/shard_map/all_to_all | solution.py:577
  97.1 0.7 pad_add_fusion.at_ref
  97.8 9.6 %all-to-all-done.2.got_ref.e_ref = f32[32,3,8,128]{3,2,1,0:T(8,128)S(1)} async-done(((f32[32,3,8,128]{3,2,1,0:T(8,128)}), f32[32,3,8,128]{3,2,1,0:T(8,128)S(1)}, u32[]{:S(2)}, u32[]{:S(2)}) %all-to-all-start.2) | async-done | bytes 393248 | tf_op jit(solution)/shard_map/all_to_all | solution.py:577
  107.4 0.8 copy-done.29
  108.3 0.7 copy-done.30
  108.9 0.6 shard_map.77
  109.6 1.3 collective-permute-start.6
  110.9 4.4 %collective-permute-start.7 = (f32[2,8,8,128]{3,2,1,0:T(8,128)S(1)}, f32[2,8,8,128]{3,2,1,0:T(8,128)S(1)}, u32[]{:S(2)}, u32[]{:S(2)}) collective-permute-start(f32[2,8,8,128]{3,2,1,0:T(8,128)S(1)} %shard_map.77), channel_id=1, source_target_pairs={{0,8},{8,16},{16,24},{24,32},{32,40},{40,48},{48,56},{56,64},{64,7... | collective-permute-start | bytes 196616 | tf_op jit(solution)/shard_map/ppermute | solution.py:515
  115.3 0.2 collective-permute-done.6
  115.5 1.1 collective-permute-done.7
  116.6 0.7 select_bitcast_fusion.1
  117.3 3.1 %collective-permute-start.8 = (f32[2,4,2,8,128]{4,3,1,0,2:T(8,128)S(1)}, f32[2,4,2,8,128]{4,3,1,0,2:T(8,128)S(1)}, u32[]{:S(2)}, u32[]{:S(2)}) collective-permute-start(f32[2,4,2,8,128]{4,3,1,0,2:T(8,128)S(1)} %get-tuple-element.56), channel_id=1, source_target_pairs={{1,0},{2,1},{3,2},{4,3},{5,4},{6,5},{7,6},{9,8},{10,9},{11,10},{12... | collective-permute-start | bytes 196616 | tf_op jit(solution)/shard_map/ppermute | solution.py:516
  120.4 2.4 %collective-permute-start.9 = (f32[2,4,2,8,128]{4,3,1,0,2:T(8,128)S(1)}, f32[2,4,2,8,128]{4,3,1,0,2:T(8,128)S(1)}, u32[]{:S(2)}, u32[]{:S(2)}) collective-permute-start(f32[2,4,2,8,128]{4,3,1,0,2:T(8,128)S(1)} %get-tuple-element.55), channel_id=1, source_target_pairs={{0,1},{1,2},{2,3},{3,4},{4,5},{5,6},{6,7},{8,9},{9,10},{10,11},{11... | collective-permute-start | bytes 196616 | tf_op jit(solution)/shard_map/ppermute | solution.py:515
  122.9 1.2 collective-permute-done.9
  124.2 0.7 copy-done.15
  125.0 0.7 copy-done.17
  125.7 0.7 copy-done.21
  126.4 0.7 copy-done.23
  127.1 1.1 shard_map.78
  128.2 1.3 collective-permute-start.10
  129.5 4.0 %collective-permute-start.11 = (f32[8,8,128]{2,1,0:T(8,128)S(1)}, f32[8,8,128]{2,1,0:T(8,128)S(1)}, u32[]{:S(2)}, u32[]{:S(2)}) collective-permute-start(f32[8,8,128]{2,1,0:T(8,128)S(1)} %get-tuple-element.36), channel_id=1, source_target_pairs={{0,128},{128,256},{256,384},{1,129},{129,257},{257,385},{2,130},{1... | collective-permute-start | bytes 98312 | tf_op jit(solution)/shard_map/ppermute | solution.py:515
  133.5 1.0 collective-permute-done.11
  134.5 1.3 collective-permute-start.12
  135.8 4.4 %collective-permute-start.13 = (f32[2,8,8,128]{3,2,1,0:T(8,128)S(1)}, f32[2,8,8,128]{3,2,1,0:T(8,128)S(1)}, u32[]{:S(2)}, u32[]{:S(2)}) collective-permute-start(f32[2,8,8,128]{3,2,1,0:T(8,128)S(1)} %get-tuple-element.61), channel_id=1, source_target_pairs={{0,8},{8,16},{16,24},{24,32},{32,40},{40,48},{48,56},{56,64},{64,7... | collective-permute-start | bytes 196616 | tf_op jit(solution)/shard_map/ppermute | solution.py:515
  140.3 1.3 collective-permute-done.13
  141.6 0.1 select_bitcast_fusion
  141.7 3.6 %collective-permute-start.14 = (f32[2,4,2,8,128]{4,3,2,1,0:T(8,128)S(1)}, f32[2,4,2,8,128]{4,3,2,1,0:T(8,128)S(1)}, u32[]{:S(2)}, u32[]{:S(2)}) collective-permute-start(f32[2,4,2,8,128]{4,3,2,1,0:T(8,128)S(1)} %get-tuple-element.54), channel_id=1, source_target_pairs={{1,0},{2,1},{3,2},{4,3},{5,4},{6,5},{7,6},{9,8},{10,9},{11,10},{12... | collective-permute-start | bytes 196616 | tf_op jit(solution)/shard_map/ppermute | solution.py:516
  145.3 4.6 %collective-permute-start.15 = (f32[2,4,2,8,128]{4,3,2,1,0:T(8,128)S(1)}, f32[2,4,2,8,128]{4,3,2,1,0:T(8,128)S(1)}, u32[]{:S(2)}, u32[]{:S(2)}) collective-permute-start(f32[2,4,2,8,128]{4,3,2,1,0:T(8,128)S(1)} %get-tuple-element.53), channel_id=1, source_target_pairs={{0,1},{1,2},{2,3},{3,4},{4,5},{5,6},{6,7},{8,9},{9,10},{10,11},{11... | collective-permute-start | bytes 196616 | tf_op jit(solution)/shard_map/ppermute | solution.py:515
  149.9 1.3 collective-permute-done.15.down_ref
  151.2 0.7 shard_map.79
  151.9 15.2 %all_to_all.27.got_ref = f32[32,8,128]{2,1,0:T(8,128)S(1)} all-to-all(f32[32,8,128]{2,1,0:T(8,128)S(1)} %get-tuple-element.37), channel_id=1, replica_groups=mesh['gx'=4,'gy'=16,'gz'=8] {'gx','gz'}, dimensions={0} | all-to-all | bytes 262144 | tf_op jit(solution)/shard_map/all_to_all | solution.py:597
  167.1 0.1 shard_map.80
  167.1 22.3 %all_to_all.28.got_ref = f32[16,8,128]{2,1,0:T(8,128)S(1)} all-to-all(f32[16,8,128]{2,1,0:T(8,128)S(1)} %shard_map.80), channel_id=1, replica_groups=mesh['gx'=4,'gy'=16,'gz'=8] {'gy'}, dimensions={0} | all-to-all | bytes 131072 | tf_op jit(solution)/shard_map/all_to_all | solution.py:599
  189.4 1.4 shard_map.81
  (102 shorter events, 0.6 us)
Async XLA Ops:
  0.0 1.0 copy-start.12
  1.0 0.8 copy-start.26
  1.8 0.8 copy-start.27
  2.6 0.7 copy-start.31
  3.2 0.7 copy-start.32
  5.6 6.3 %collective-permute-start = (f32[29,8,128]{2,1,0:T(8,128)S(1)}, f32[29,8,128]{2,1,0:T(8,128)S(1)}, u32[]{:S(2)}, u32[]{:S(2)}) collective-permute-start(f32[29,8,128]{2,1,0:T(8,128)S(1)} %pad_maximum_fusion.13), channel_id=1, source_target_pairs={{128,0},{256,128},{384,256},{129,1},{257,129},{385,257},{130,2},{2... | collective-permute-start | bytes 356360 | tf_op jit(solution)/shard_map/ppermute | solution.py:516
  6.9 6.5 %collective-permute-start.1 = (f32[29,8,128]{2,1,0:T(8,128)S(1)}, f32[29,8,128]{2,1,0:T(8,128)S(1)}, u32[]{:S(2)}, u32[]{:S(2)}) collective-permute-start(f32[29,8,128]{2,1,0:T(8,128)S(1)} %pad_maximum_fusion.13), channel_id=1, source_target_pairs={{0,128},{128,256},{256,384},{1,129},{129,257},{257,385},{2,130},{1... | collective-permute-start | bytes 356360 | tf_op jit(solution)/shard_map/ppermute | solution.py:515
  11.6 1.9 %copy-start.35 = (pred[128]{0:T(512)(128)(4,1)}, pred[128]{0:T(512)(128)(4,1)S(1)}, u32[]{:S(2)}) copy-start(pred[128]{0:T(512)(128)(4,1)S(1)} %iota_compare_fusion.1) | copy-start | bytes 388
  11.7 45.0 %copy-start.33 = (pred[8]{0:T(512)(128)(4,1)}, pred[8]{0:T(512)(128)(4,1)S(1)}, u32[]{:S(2)}) copy-start(pred[8]{0:T(512)(128)(4,1)S(1)} %iota_compare_fusion) | copy-start | bytes 28
  13.6 8.2 %collective-permute-start.2 = (f32[81,8,128]{2,1,0:T(8,128)S(1)}, f32[81,8,128]{2,1,0:T(8,128)S(1)}, u32[]{:S(2)}, u32[]{:S(2)}) collective-permute-start(f32[81,8,128]{2,1,0:T(8,128)S(1)} %get-tuple-element.47), channel_id=1, source_target_pairs={{8,0},{16,8},{24,16},{32,24},{40,32},{48,40},{56,48},{64,56},{72,6... | collective-permute-start | bytes 995336 | tf_op jit(solution)/shard_map/ppermute | solution.py:516
  14.9 8.4 %collective-permute-start.3 = (f32[81,8,128]{2,1,0:T(8,128)S(1)}, f32[81,8,128]{2,1,0:T(8,128)S(1)}, u32[]{:S(2)}, u32[]{:S(2)}) collective-permute-start(f32[81,8,128]{2,1,0:T(8,128)S(1)} %get-tuple-element.48), channel_id=1, source_target_pairs={{0,8},{8,16},{16,24},{24,32},{32,40},{40,48},{48,56},{56,64},{64,7... | collective-permute-start | bytes 995336 | tf_op jit(solution)/shard_map/ppermute | solution.py:515
  19.3 67.3 %copy-start.16 = (f32[32,128]{1,0:T(8,128)}, f32[32,128]{1,0:T(8,128)S(1)}, u32[]{:S(2)}) copy-start(f32[32,128]{1,0:T(8,128)S(1)} %slice_bitcast_fusion.1.fxl_ref.fxl) | copy-start | bytes 49156
  23.4 12.9 %collective-permute-start.4 = (f32[81,8,128]{2,1,0:T(8,128)S(1)}, f32[81,8,128]{2,1,0:T(8,128)S(1)}, u32[]{:S(2)}, u32[]{:S(2)}) collective-permute-start(f32[81,8,128]{2,1,0:T(8,128)S(1)} %get-tuple-element.65), channel_id=1, source_target_pairs={{1,0},{2,1},{3,2},{4,3},{5,4},{6,5},{7,6},{9,8},{10,9},{11,10},{12... | collective-permute-start | bytes 995336 | tf_op jit(solution)/shard_map/ppermute | solution.py:516
  33.5 6.0 %collective-permute-start.5 = (f32[81,8,128]{2,1,0:T(8,128)S(1)}, f32[81,8,128]{2,1,0:T(8,128)S(1)}, u32[]{:S(2)}, u32[]{:S(2)}) collective-permute-start(f32[81,8,128]{2,1,0:T(8,128)S(1)} %get-tuple-element.64), channel_id=1, source_target_pairs={{0,1},{1,2},{2,3},{3,4},{4,5},{5,6},{6,7},{8,9},{9,10},{10,11},{11... | collective-permute-start | bytes 995336 | tf_op jit(solution)/shard_map/ppermute | solution.py:515
  35.4 51.1 %copy-start.1 = (f32[32,8,128]{2,1,0:T(8,128)}, f32[32,8,128]{2,1,0:T(8,128)S(1)}, u32[]{:S(2)}) copy-start(f32[32,8,128]{2,1,0:T(8,128)S(1)} %slice.157) | copy-start | bytes 393220
  35.4 51.1 %copy-start.3 = (f32[32,8,128]{2,1,0:T(8,128)}, f32[32,8,128]{2,1,0:T(8,128)S(1)}, u32[]{:S(2)}) copy-start(f32[32,8,128]{2,1,0:T(8,128)S(1)} %slice.158) | copy-start | bytes 393220
  39.5 47.1 %copy-start.20 = (f32[8,128]{1,0:T(8,128)}, f32[8,128]{1,0:T(8,128)S(1)}, u32[]{:S(2)}) copy-start(f32[8,128]{1,0:T(8,128)S(1)} %concatenate.43.owners_ref) | copy-start | bytes 12292
  39.5 47.0 %copy-start = (f32[256,256]{1,0:T(8,128)S(1)}, f32[256,256]{1,0:T(8,128)}, u32[]{:S(2)}) copy-start(f32[256,256]{1,0:T(8,128)} %cinv_ref.5) | copy-start | bytes 786436
  39.5 47.6 %copy-start.5 = (f32[32,8,128]{2,1,0:T(8,128)}, f32[32,8,128]{2,1,0:T(8,128)S(1)}, u32[]{:S(2)}) copy-start(f32[32,8,128]{2,1,0:T(8,128)S(1)} %slice.159) | copy-start | bytes 393220
  39.6 47.6 %copy-start.7 = (f32[32,8,128]{2,1,0:T(8,128)}, f32[32,8,128]{2,1,0:T(8,128)S(1)}, u32[]{:S(2)}) copy-start(f32[32,8,128]{2,1,0:T(8,128)S(1)} %slice.160) | copy-start | bytes 393220
  39.6 1.1 copy-start.9
  43.1 44.1 %copy-start.10 = (f32[10,16,256]{2,1,0:T(8,128)}, f32[10,16,256]{2,1,0:T(8,128)S(1)}, u32[]{:S(2)}) copy-start(f32[10,16,256]{2,1,0:T(8,128)S(1)} %get-tuple-element.30.s_ref) | copy-start | bytes 491524
  43.1 44.1 %copy-start.14 = (f32[8,8,128]{2,1,0:T(8,128)}, f32[8,8,128]{2,1,0:T(8,128)S(1)}, u32[]{:S(2)}) copy-start(f32[8,8,128]{2,1,0:T(8,128)S(1)} %get-tuple-element.29.d_ref) | copy-start | bytes 98308
  43.1 44.1 %copy-start.18 = (f32[16,16,256]{2,1,0:T(8,128)}, f32[16,16,256]{2,1,0:T(8,128)S(1)}, u32[]{:S(2)}) copy-start(f32[16,16,256]{2,1,0:T(8,128)S(1)} %get-tuple-element.33.b4_ref) | copy-start | bytes 786436
  87.2 0.8 copy-start.13
  87.9 0.6 copy-start.22
  88.5 0.6 copy-start.24
  89.1 0.6 copy-start.28
  89.8 17.6 %all-to-all-start.2 = ((f32[32,3,8,128]{3,2,1,0:T(8,128)}), f32[32,3,8,128]{3,2,1,0:T(8,128)S(1)}, u32[]{:S(2)}, u32[]{:S(2)}) async-start(f32[32,3,8,128]{3,2,1,0:T(8,128)} %copy-done.13), calls=%async_computation.2 | async-start | bytes 786432 | tf_op jit(solution)/shard_map/all_to_all | solution.py:577
  107.4 16.8 %copy-start.2 = (f32[32,8,128]{2,1,0:T(8,128)S(1)}, f32[32,8,128]{2,1,0:T(8,128)}, u32[]{:S(2)}) copy-start(f32[32,8,128]{2,1,0:T(8,128)} %copy-done.1) | copy-start | bytes 393220
  107.4 16.8 %copy-start.4 = (f32[32,8,128]{2,1,0:T(8,128)S(1)}, f32[32,8,128]{2,1,0:T(8,128)}, u32[]{:S(2)}) copy-start(f32[32,8,128]{2,1,0:T(8,128)} %copy-done.3) | copy-start | bytes 393220
  107.4 16.8 %copy-start.6 = (f32[32,8,128]{2,1,0:T(8,128)S(1)}, f32[32,8,128]{2,1,0:T(8,128)}, u32[]{:S(2)}) copy-start(f32[32,8,128]{2,1,0:T(8,128)} %copy-done.5) | copy-start | bytes 393220
  107.4 16.8 %copy-start.8 = (f32[32,8,128]{2,1,0:T(8,128)S(1)}, f32[32,8,128]{2,1,0:T(8,128)}, u32[]{:S(2)}) copy-start(f32[32,8,128]{2,1,0:T(8,128)} %copy-done.7) | copy-start | bytes 393220
  107.4 16.8 %copy-start.11 = (f32[10,16,256]{2,1,0:T(8,128)S(1)}, f32[10,16,256]{2,1,0:T(8,128)}, u32[]{:S(2)}) copy-start(f32[10,16,256]{2,1,0:T(8,128)} %copy-done.10) | copy-start | bytes 491524
  107.4 16.8 %copy-start.19 = (f32[16,16,256]{2,1,0:T(8,128)S(1)}, f32[16,16,256]{2,1,0:T(8,128)}, u32[]{:S(2)}) copy-start(f32[16,16,256]{2,1,0:T(8,128)} %copy-done.18) | copy-start | bytes 786436
  107.4 0.8 copy-start.29
  108.3 0.7 copy-start.30
  109.6 6.0 %collective-permute-start.6 = (f32[2,8,8,128]{3,2,1,0:T(8,128)S(1)}, f32[2,8,8,128]{3,2,1,0:T(8,128)S(1)}, u32[]{:S(2)}, u32[]{:S(2)}) collective-permute-start(f32[2,8,8,128]{3,2,1,0:T(8,128)S(1)} %shard_map.77), channel_id=1, source_target_pairs={{8,0},{16,8},{24,16},{32,24},{40,32},{48,40},{56,48},{64,56},{72,6... | collective-permute-start | bytes 196616 | tf_op jit(solution)/shard_map/ppermute | solution.py:516
  110.9 5.7 %collective-permute-start.7 = (f32[2,8,8,128]{3,2,1,0:T(8,128)S(1)}, f32[2,8,8,128]{3,2,1,0:T(8,128)S(1)}, u32[]{:S(2)}, u32[]{:S(2)}) collective-permute-start(f32[2,8,8,128]{3,2,1,0:T(8,128)S(1)} %shard_map.77), channel_id=1, source_target_pairs={{0,8},{8,16},{16,24},{24,32},{32,40},{40,48},{48,56},{56,64},{64,7... | collective-permute-start | bytes 196616 | tf_op jit(solution)/shard_map/ppermute | solution.py:515
  117.3 5.6 %collective-permute-start.8 = (f32[2,4,2,8,128]{4,3,1,0,2:T(8,128)S(1)}, f32[2,4,2,8,128]{4,3,1,0,2:T(8,128)S(1)}, u32[]{:S(2)}, u32[]{:S(2)}) collective-permute-start(f32[2,4,2,8,128]{4,3,1,0,2:T(8,128)S(1)} %get-tuple-element.56), channel_id=1, source_target_pairs={{1,0},{2,1},{3,2},{4,3},{5,4},{6,5},{7,6},{9,8},{10,9},{11,10},{12... | collective-permute-start | bytes 196616 | tf_op jit(solution)/shard_map/ppermute | solution.py:516
  120.4 3.8 %collective-permute-start.9 = (f32[2,4,2,8,128]{4,3,1,0,2:T(8,128)S(1)}, f32[2,4,2,8,128]{4,3,1,0,2:T(8,128)S(1)}, u32[]{:S(2)}, u32[]{:S(2)}) collective-permute-start(f32[2,4,2,8,128]{4,3,1,0,2:T(8,128)S(1)} %get-tuple-element.55), channel_id=1, source_target_pairs={{0,1},{1,2},{2,3},{3,4},{4,5},{5,6},{6,7},{8,9},{9,10},{10,11},{11... | collective-permute-start | bytes 196616 | tf_op jit(solution)/shard_map/ppermute | solution.py:515
  124.2 0.8 copy-start.15
  125.0 0.7 copy-start.17
  125.7 0.7 copy-start.21
  126.4 0.7 copy-start.23
  127.1 7.4 %copy-start.36 = (pred[128]{0:T(512)(128)(4,1)S(1)}, pred[128]{0:T(512)(128)(4,1)}, u32[]{:S(2)}) copy-start(pred[128]{0:T(512)(128)(4,1)} %copy-done.35) | copy-start | bytes 388
  127.1 14.5 %copy-start.34 = (pred[8]{0:T(512)(128)(4,1)S(1)}, pred[8]{0:T(512)(128)(4,1)}, u32[]{:S(2)}) copy-start(pred[8]{0:T(512)(128)(4,1)} %copy-done.33) | copy-start | bytes 28
  128.2 5.3 %collective-permute-start.10 = (f32[8,8,128]{2,1,0:T(8,128)S(1)}, f32[8,8,128]{2,1,0:T(8,128)S(1)}, u32[]{:S(2)}, u32[]{:S(2)}) collective-permute-start(f32[8,8,128]{2,1,0:T(8,128)S(1)} %get-tuple-element.36), channel_id=1, source_target_pairs={{128,0},{256,128},{384,256},{129,1},{257,129},{385,257},{130,2},{2... | collective-permute-start | bytes 98312 | tf_op jit(solution)/shard_map/ppermute | solution.py:516
  129.5 5.0 %collective-permute-start.11 = (f32[8,8,128]{2,1,0:T(8,128)S(1)}, f32[8,8,128]{2,1,0:T(8,128)S(1)}, u32[]{:S(2)}, u32[]{:S(2)}) collective-permute-start(f32[8,8,128]{2,1,0:T(8,128)S(1)} %get-tuple-element.36), channel_id=1, source_target_pairs={{0,128},{128,256},{256,384},{1,129},{129,257},{257,385},{2,130},{1... | collective-permute-start | bytes 98312 | tf_op jit(solution)/shard_map/ppermute | solution.py:515
  134.5 5.8 %collective-permute-start.12 = (f32[2,8,8,128]{3,2,1,0:T(8,128)S(1)}, f32[2,8,8,128]{3,2,1,0:T(8,128)S(1)}, u32[]{:S(2)}, u32[]{:S(2)}) collective-permute-start(f32[2,8,8,128]{3,2,1,0:T(8,128)S(1)} %get-tuple-element.61), channel_id=1, source_target_pairs={{8,0},{16,8},{24,16},{32,24},{40,32},{48,40},{56,48},{64,56},{72,6... | collective-permute-start | bytes 196616 | tf_op jit(solution)/shard_map/ppermute | solution.py:516
  135.8 5.8 %collective-permute-start.13 = (f32[2,8,8,128]{3,2,1,0:T(8,128)S(1)}, f32[2,8,8,128]{3,2,1,0:T(8,128)S(1)}, u32[]{:S(2)}, u32[]{:S(2)}) collective-permute-start(f32[2,8,8,128]{3,2,1,0:T(8,128)S(1)} %get-tuple-element.61), channel_id=1, source_target_pairs={{0,8},{8,16},{16,24},{24,32},{32,40},{40,48},{48,56},{56,64},{64,7... | collective-permute-start | bytes 196616 | tf_op jit(solution)/shard_map/ppermute | solution.py:515
  141.7 8.2 %collective-permute-start.14 = (f32[2,4,2,8,128]{4,3,2,1,0:T(8,128)S(1)}, f32[2,4,2,8,128]{4,3,2,1,0:T(8,128)S(1)}, u32[]{:S(2)}, u32[]{:S(2)}) collective-permute-start(f32[2,4,2,8,128]{4,3,2,1,0:T(8,128)S(1)} %get-tuple-element.54), channel_id=1, source_target_pairs={{1,0},{2,1},{3,2},{4,3},{5,4},{6,5},{7,6},{9,8},{10,9},{11,10},{12... | collective-permute-start | bytes 196616 | tf_op jit(solution)/shard_map/ppermute | solution.py:516
  145.3 5.9 %collective-permute-start.15 = (f32[2,4,2,8,128]{4,3,2,1,0:T(8,128)S(1)}, f32[2,4,2,8,128]{4,3,2,1,0:T(8,128)S(1)}, u32[]{:S(2)}, u32[]{:S(2)}) collective-permute-start(f32[2,4,2,8,128]{4,3,2,1,0:T(8,128)S(1)} %get-tuple-element.53), channel_id=1, source_target_pairs={{0,1},{1,2},{2,3},{3,4},{4,5},{5,6},{6,7},{8,9},{9,10},{10,11},{11... | collective-permute-start | bytes 196616 | tf_op jit(solution)/shard_map/ppermute | solution.py:515
  151.2 38.2 %copy-start.25 = (f32[8,8,128]{2,1,0:T(8,128)S(1)}, f32[8,8,128]{2,1,0:T(8,128)}, u32[]{:S(2)}) copy-start(f32[8,8,128]{2,1,0:T(8,128)} %copy-done.24) | copy-start | bytes 98308

commit v2 on v1

--- a/solution.py
+++ b/solution.py
@@ -1,5 +1,3 @@
-import functools
-
 import jax
 import jax.numpy as jnp
 from jax import lax
@@ -13,18 +11,19 @@
 F32 = jnp.float32
 PLANE = ("gx", "gz")
 VM = pl.BlockSpec(memory_space=pltpu.VMEM)
-SM = pl.BlockSpec(memory_space=pltpu.SMEM)
-
-
-def call(body, outs, ins, scratch=(), smem=()):
+X_FACE, Y_FACE, Z_FACE = 3, 15, 30
+X_OWN, Y_OWN, Z_OWN = 7, 47, 62
+
+
+def call(body, outs, ins, scratch=(), hbm=False, vmem=6):
     single = isinstance(outs[0], int)
     shapes = [outs] if single else outs
     shapes = [jax.ShapeDtypeStruct(s, F32) for s in shapes]
-    specs = [SM if i in smem else VM for i in range(len(ins))]
     res = pl.pallas_call(
-        body, out_shape=shapes, in_specs=specs, out_specs=[VM] * len(shapes),
-        scratch_shapes=[pltpu.VMEM(s, d) for s, d in scratch],
-        compiler_params=pltpu.CompilerParams(vmem_limit_bytes=40 * 2**20),
+        body, out_shape=shapes,
+        in_specs=[pl.BlockSpec(memory_space=pltpu.HBM) if hbm else VM] * len(ins),
+        out_specs=[VM] * len(shapes), scratch_shapes=list(scratch),
+        compiler_params=pltpu.CompilerParams(vmem_limit_bytes=vmem * 2**20),
     )(*ins)
     return res[0] if single else res
 
@@ -86,8 +85,10 @@
     return [jnp.sum(bt_ref[z * 8:z * 8 + 8] * c[None], axis=1) for z in range(8)]
 
 
-def face_value(f_ref, col):
-    return jnp.sum(f_ref[...] * jnp.broadcast_to(col, (BASIS, 128))[None], axis=1)
+def face_value(ref, start, col):
+    c = jnp.broadcast_to(col, (BASIS, 128))
+    rows = [jnp.sum(block(ref, start + 4 * i) * c, axis=0, keepdims=True) for i in range(8)]
+    return jnp.concatenate(rows, axis=0)
 
 
 def line_value(fx, col):
@@ -95,13 +96,13 @@
 
 
 def prolong(bt_ref, faces, own_rows, vrow):
-    fxl, fxr, fym, fyp, fzm, fzp = faces
+    lx, rx, yb, ya, zb, za = faces
     cols = [near_column(vrow, o) for o in own_rows]
     mine = brick_value(bt_ref, cols[0])
-    left = spread(line_value(fxl[...], cols[1]), 8)
-    right = spread(line_value(fxr[...], cols[2]), 8)
-    ym, yp = face_value(fym, cols[3]), face_value(fyp, cols[4])
-    zm, zp = face_value(fzm, cols[5]), face_value(fzp, cols[6])
+    left = spread(line_value(block(lx, X_FACE), cols[1]), 8)
+    right = spread(line_value(block(rx, X_FACE), cols[2]), 8)
+    ym, yp = face_value(yb, Y_FACE, cols[3]), face_value(ya, Y_FACE, cols[4])
+    zm, zp = face_value(zb, Z_FACE, cols[5]), face_value(za, Z_FACE, cols[6])
     sub, lane = iota((8, 128), 0), iota((8, 128), 1)
     zero = jnp.zeros((8, 128), F32)
     planes = {}
@@ -143,18 +144,65 @@
         d_ref[z] * (s[z] - (1 / RELAX) * around(c_ref, s, z))[:8, :128] for z in range(8)]
 
 
-def plane_of(own_ref, up_ref, down_ref, z, *lead):
-    if z < 0:
-        ref, i = down_ref, z + 4
-    elif z >= 8:
-        ref, i = up_ref, z - 8
-    else:
-        ref, i = own_ref, z
-    t = [[ref[lead + (x, i, y)] for x in range(2)] for y in range(2)]
-    return jnp.concatenate([jnp.concatenate(t[0], axis=1), jnp.concatenate(t[1], axis=1)], axis=0)
-
-
-def first_body(perm_ref, store_ref, b_ref, cls_ref, basis_ref, f_ref, bt_ref, fx_ref):
+def square(own, beyond, m, my, z):
+    lane = iota((8, 128), 1)
+    edge = (lane < 4) | (lane >= 124)
+    shift = (124 - 8 * z) % 128
+    side = jnp.where(edge, pltpu.roll(m, shift, 1), 0.0)
+    corner = jnp.where(edge, pltpu.roll(my, (shift + 64) % 128, 1), 0.0)
+    return jnp.concatenate([
+        jnp.concatenate([own, side], axis=1), jnp.concatenate([beyond, corner], axis=1)], axis=0)
+
+
+def pack(planes, start=0):
+    lane = iota((8, 128), 1)
+    out = jnp.zeros((8, 128), F32)
+    for z in range(8):
+        out = jnp.where(
+            lane // 8 == z + start // 8, pltpu.roll(planes[z], 4 + 8 * z + start, 1), out)
+    return out
+
+
+def meet(left, right):
+    return jnp.where(iota((8, 128), 1) % 8 < 4, left, right)
+
+
+def upper(planes):
+    half = iota((8, 128), 0) < 4
+    return [jnp.where(half, pltpu.roll(planes[2 * i], 4, 0), planes[2 * i + 1]) for i in range(4)]
+
+
+def lower(planes):
+    half = iota((8, 128), 0) < 4
+    return [jnp.where(half, planes[2 * i], pltpu.roll(planes[2 * i + 1], 4, 0)) for i in range(4)]
+
+
+def beyond_y(above, below):
+    half = iota((8, 128), 0) < 4
+    out = []
+    for i in range(4):
+        out.append(jnp.where(half, above[i], pltpu.roll(below[i], 4, 0)))
+        out.append(jnp.where(half, pltpu.roll(above[i], 4, 0), below[i]))
+    return out
+
+
+def both(m, my):
+    return jnp.where(iota((8, 128), 1) < 64, m, pltpu.roll(my, 64, 1))
+
+
+def block(ref, start):
+    return jnp.concatenate([ref[start + i] for i in range(4)], axis=0)
+
+
+def first_body(perm_hbm, store_hbm, b_hbm, cls_hbm, basis_hbm, owner_hbm, f_ref, bt_ref, msg_ref,
+               perm_ref, store_ref, b_ref, cls_ref, basis_ref, owner_ref, sems):
+    copies = [pltpu.make_async_copy(src, dst, sems.at[i]) for i, (src, dst) in enumerate((
+        (perm_hbm, perm_ref), (store_hbm, store_ref), (owner_hbm, owner_ref), (cls_hbm, cls_ref),
+        (b_hbm, b_ref), (basis_hbm, basis_ref)))]
+    for c in copies:
+        c.start()
+    for c in copies[:5]:
+        c.wait()
     ks, sts = [], []
     for z in range(8):
         c = cls_ref[z]
@@ -175,6 +223,17 @@
         down = pltpu.roll(up, 1, 0)
         f_ref[3, z] = sts[z] + jnp.where(sub == 3, up, jnp.where(sub == 4, down, 0.0))
         f_ref[4, z] = sts[z] + tz if z in (3, 4) else sts[z]
+    msg_ref[0] = pack([b_ref[z] for z in range(8)])
+    msg_ref[1] = pack(ks)
+    lane8 = iota((8, 128), 1)
+    stx = []
+    for z in range(8):
+        face = harmonic(ks[z], pltpu.roll(ks[z], 127, 1))
+        stx.append(sts[z] + jnp.where(
+            lane8 == 3, face, jnp.where(lane8 == 124, pltpu.roll(face, 1, 1), 0.0)))
+    msg_ref[2] = pack(stx)
+    msg_ref[X_OWN] = jnp.broadcast_to(owner_ref[0].astype(F32), (8, 128))
+    copies[5].wait()
     lane = iota((BASIS, 128), 1)
     lo = jnp.zeros((BASIS, 128), F32)
     hi = jnp.zeros((BASIS, 128), F32)
@@ -186,17 +245,75 @@
             r = pltpu.roll(t[y], i, 1) if i else t[y]
             lo = jnp.where(lane == i, r, lo)
             hi = jnp.where(lane == (i - 1) % 128, r, hi)
-    fx_ref[...] = jnp.where(lane < 64, lo, pltpu.roll(hi, 65, 1))
-
-
-def setup_body(own_ref, up_ref, down_ref, owners_ref, bt_ref, fx_ref, fxl_ref, fxr_ref, fym_ref,
-               fyp_ref, fzm_ref, fzp_ref, c_ref, d_ref, s_ref, b4_ref, msg_ref, k_ref, t_ref,
-               bf_ref, wh_ref, wl_ref):
+    fx = jnp.where(lane < 64, lo, pltpu.roll(hi, 65, 1))
+    for i in range(4):
+        msg_ref[X_FACE + i] = fx[8 * i:8 * i + 8]
+
+
+def beside_body(left_ref, right_ref, mine_ref, f_ref, bt_ref, m_ref, up_ref, down_ref):
+    for f, src in enumerate((0, 1, 3)):
+        planes = [f_ref[src, z] for z in range(8)]
+        m = meet(left_ref[f], right_ref[f])
+        m_ref[f] = m
+        for i, (u, d) in enumerate(zip(upper(planes), lower(planes))):
+            up_ref[4 * f + i] = u
+            down_ref[4 * f + i] = d
+        up_ref[12 + f] = m
+        down_ref[12 + f] = m
+    for z in range(8):
+        for i in range(4):
+            up_ref[Y_FACE + 4 * z + i] = bt_ref[8 * z + 7, 8 * i:8 * i + 8]
+            down_ref[Y_FACE + 4 * z + i] = bt_ref[8 * z, 8 * i:8 * i + 8]
+    up_ref[Y_OWN] = mine_ref[X_OWN]
+    down_ref[Y_OWN] = mine_ref[X_OWN]
+
+
+def beyond_body(below_ref, above_ref, mine_ref, f_ref, bt_ref, m_ref, y_ref, mb_ref, up_ref, down_ref):
+    half = iota((8, 128), 0) < 4
+    for f, src in enumerate((0, 1, 4)):
+        y = beyond_y([above_ref[4 * f + i] for i in range(4)], [below_ref[4 * f + i] for i in range(4)])
+        for z in range(8):
+            y_ref[f, z] = y[z]
+        for i in range(4):
+            up_ref[8 * f + 2 * i] = f_ref[src, 4 + i]
+            up_ref[8 * f + 2 * i + 1] = y[4 + i]
+            down_ref[8 * f + 2 * i] = f_ref[src, i]
+            down_ref[8 * f + 2 * i + 1] = y[i]
+        m = both(m_ref[f], jnp.where(half, above_ref[12 + f], below_ref[12 + f]))
+        mb_ref[f] = m
+        up_ref[24 + f] = m
+        down_ref[24 + f] = m
+    zero = jnp.zeros((8, 128), F32)
+    for i in range(3):
+        up_ref[27 + i] = zero
+        down_ref[27 + i] = zero
+    for y in range(8):
+        for i in range(4):
+            up_ref[Z_FACE + 4 * y + i] = bt_ref[56 + y, 8 * i:8 * i + 8]
+            down_ref[Z_FACE + 4 * y + i] = bt_ref[y, 8 * i:8 * i + 8]
+    up_ref[Z_OWN] = mine_ref[X_OWN]
+    down_ref[Z_OWN] = mine_ref[X_OWN]
+
+
+def setup_body(f_ref, y_ref, mb_ref, zb_ref, za_ref, lx_ref, rx_ref, yb_ref, ya_ref, mine_ref, bt_ref,
+               c_ref, d_ref, s_ref, b4_ref, msg_ref, owners_ref, k_ref, t_ref, bf_ref, wh_ref, wl_ref):
+    def plane(f, z):
+        if 0 <= z < 8:
+            m = mb_ref[f]
+            return square(f_ref[f, z], y_ref[f, z], m, m, z)
+        ref, i, at = (za_ref, z - 8, z - 8) if z >= 8 else (zb_ref, z + 4, z + 8)
+        m = ref[24 + f]
+        return square(ref[8 * f + 2 * i], ref[8 * f + 2 * i + 1], m, m, at)
+
+    for i, ref, at in ((0, mine_ref, X_OWN), (1, lx_ref, X_OWN), (2, rx_ref, X_OWN), (3, yb_ref, Y_OWN),
+                       (4, ya_ref, Y_OWN), (5, zb_ref, Z_OWN), (6, za_ref, Z_OWN)):
+        owners_ref[i:i + 1, :] = ref[at][0:1, :]
+    owners_ref[7:8, :] = mine_ref[X_OWN][0:1, :]
     lane = iota((16, 256), 1)
     sub = iota((16, 256), 0)
     for z in range(-4, 12):
-        k_ref[z % 16] = plane_of(own_ref, up_ref, down_ref, z, 1)
-        b4_ref[z % 16] = plane_of(own_ref, up_ref, down_ref, z, 0)
+        k_ref[z % 16] = plane(1, z)
+        b4_ref[z % 16] = plane(0, z)
     for z in range(-4, 12):
         p = z % 16
         k = k_ref[p]
@@ -210,7 +327,7 @@
         p = z % 16
         tx, ty, tz = t_ref[0, p], t_ref[1, p], t_ref[2, p]
         xm, ym, zm = pltpu.roll(tx, 1, 1), pltpu.roll(ty, 1, 0), t_ref[2, (z - 1) % 16]
-        st = plane_of(own_ref, up_ref, down_ref, z, 2)
+        st = plane(2, z)
         diag = st + (tx + xm) + (ty + ym) + (tz + zm)
         inv = jnp.where(diag > 0, 1.0 / jnp.where(diag > 0, diag, 1.0), 0.0)
         ri = RELAX * inv
@@ -281,17 +398,17 @@
 
     txl = line(lambda z: t_ref[0, z][:8, 255:256])
     txr = line(lambda z: t_ref[0, z][:8, 127:128])
-    fx = fx_ref[...]
-    blocks.append(-face(fx, txl, pltpu.roll(fxl_ref[...], 64, 1)))
-    blocks.append(-face(pltpu.roll(fx, 64, 1), txr, fxr_ref[...]))
+    fx = block(mine_ref, X_FACE)
+    blocks.append(-face(fx, txl, pltpu.roll(block(lx_ref, X_FACE), 64, 1)))
+    blocks.append(-face(pltpu.roll(fx, 64, 1), txr, block(rx_ref, X_FACE)))
     acc = jnp.zeros((4, BASIS, BASIS), F32)
     accs = [acc[0], acc[1], acc[2], acc[3]]
     for z in range(8):
-        accs[0] = accs[0] - face(bt_ref[z * 8], spread(t_ref[1, z][15:16, :128], BASIS), fym_ref[z])
-        accs[1] = accs[1] - face(bt_ref[z * 8 + 7], spread(t_ref[1, z][7:8, :128], BASIS), fyp_ref[z])
+        accs[0] = accs[0] - face(bt_ref[z * 8], spread(t_ref[1, z][15:16, :128], BASIS), block(yb_ref, Y_FACE + 4 * z))
+        accs[1] = accs[1] - face(bt_ref[z * 8 + 7], spread(t_ref[1, z][7:8, :128], BASIS), block(ya_ref, Y_FACE + 4 * z))
     for y in range(8):
-        accs[2] = accs[2] - face(bt_ref[y], spread(t_ref[2, 15][y:y + 1, :128], BASIS), fzm_ref[y])
-        accs[3] = accs[3] - face(bt_ref[56 + y], spread(t_ref[2, 7][y:y + 1, :128], BASIS), fzp_ref[y])
+        accs[2] = accs[2] - face(bt_ref[y], spread(t_ref[2, 15][y:y + 1, :128], BASIS), block(zb_ref, Z_FACE + 4 * y))
+        accs[3] = accs[3] - face(bt_ref[56 + y], spread(t_ref[2, 7][y:y + 1, :128], BASIS), block(za_ref, Z_FACE + 4 * y))
     blocks += accs
     elo = jnp.zeros((BASIS, 128), F32)
     ehi = jnp.zeros((BASIS, 128), F32)
@@ -316,7 +433,7 @@
     return jnp.where(group == o, t, 0.0), jnp.where(group + 4 == o, t, 0.0)
 
 
-def gather_body(got_ref, msg_ref, own_ref):
+def gather_body(got_ref, msg_ref):
     zero = jnp.zeros((8, 128), F32)
     elo, ehi, clo, chi, plain = zero, zero, zero, zero, zero
     sub = iota((8, 128), 0)
@@ -328,7 +445,6 @@
         ehi = ehi + jnp.where(hit, spread(t[1:2, :], 8), 0.0)
         a, b = place(t, owner)
         clo, chi, plain = clo + a, chi + b, plain + t
-        own_ref[m:m + 1, :] = owner
     row = lambda t, i: spread(t[i:i + 1, :], 8)
     rows = [row(clo, 2), row(chi, 2), row(clo, 3), row(chi, 3), row(plain, 4), row(plain, 5)]
     out = zero
@@ -348,8 +464,8 @@
     return [jnp.concatenate([owners_ref[n:n + 1, :]] * 2, axis=1) for n in range(7)]
 
 
-def begin_body(got_ref, cinv_ref, owners_ref, bt_ref, fxl, fxr, fym, fyp, fzm, fzp, c_ref, d_ref,
-               s_ref, z_ref, w_ref, msg_ref, state_ref):
+def begin_body(got_ref, cinv_ref, owners_ref, bt_ref, lx, rx, yb, ya, zb, za, c_ref, d_ref, s_ref,
+               z_ref, w_ref, up_ref, down_ref, e_ref, state_ref):
     e0 = got_ref[0, 0]
     e1 = got_ref[0, 1]
     t = got_ref[0, 2]
@@ -360,34 +476,56 @@
     state_ref[0] = t
     state_ref[1] = spread(vrow[:, :128], 8)
     state_ref[2] = spread(vrow[:, 128:], 8)
-    z = prolong(bt_ref, (fxl, fxr, fym, fyp, fzm, fzp), owner_rows(owners_ref), vrow)
+    z = prolong(bt_ref, (lx, rx, yb, ya, zb, za), owner_rows(owners_ref), vrow)
     z = {i: z[i] + s_ref[i + 1] for i in range(-1, 9)}
     w = operate(c_ref, d_ref, z)
-    lane = iota((8, 128), 1)
-    ride = jnp.zeros((8, 128), F32)
+    e_ref[0] = e0
+    e_ref[1] = e1
     for i in range(8):
         z_ref[i] = z[i][:8, :128]
         w_ref[i] = w[i]
-        ride = jnp.where(lane // 8 == i, pltpu.roll(w[i], 4 + 8 * i, 1), ride)
+    for i, (u, d) in enumerate(zip(upper(w), lower(w))):
+        up_ref[i] = u
+        down_ref[i] = d
+
+
+def ride_body(below_ref, above_ref, w_ref, e_ref, y_ref, up_ref, down_ref, msg_ref):
+    w = [w_ref[z] for z in range(8)]
+    y = beyond_y([above_ref[i] for i in range(4)], [below_ref[i] for i in range(4)])
+    for z in range(8):
+        y_ref[z] = y[z]
+    for i in range(4):
+        up_ref[2 * i], up_ref[2 * i + 1] = w[4 + i], y[4 + i]
+        down_ref[2 * i], down_ref[2 * i + 1] = w[i], y[i]
+    ride = jnp.where(iota((8, 128), 1) < 64, pack(w), pack(y, 64))
     for m in range(msg_ref.shape[0]):
-        msg_ref[m, 0] = e0
-        msg_ref[m, 1] = e1
+        msg_ref[m, 0] = e_ref[0]
+        msg_ref[m, 1] = e_ref[1]
         msg_ref[m, 2] = ride
 
 
-def ride_body(at_ref, got_ref, w_ref, out_ref):
-    left = jnp.where(at_ref[0] > 0, got_ref[jnp.maximum(at_ref[1], 0), 2], 0.0)
-    right = jnp.where(at_ref[0] < at_ref[3] - 1, got_ref[jnp.minimum(at_ref[2], BASIS - 1), 2], 0.0)
-    lane = iota((8, 128), 1)
-    for z in range(8):
-        l = pltpu.roll(left, (124 - 8 * z) % 128, 1)
-        r = pltpu.roll(right, (124 - 8 * z) % 128, 1)
-        out_ref[0, z] = w_ref[z]
-        out_ref[1, z] = jnp.where(lane < 4, r, jnp.where(lane >= 124, l, 0.0))
-
-
-def next_body(state_ref, e_ref, cinv_ref, owners_ref, bt_ref, fxl, fxr, fym, fyp, fzm, fzp, c_ref,
-              d_ref, s_ref, b4_ref, own_ref, up_ref, down_ref, z_ref, r_ref, out_ref):
+def next_body(state_ref, e_ref, cinv_ref, owners_ref, bt_ref, lx, rx, yb, ya, zb, za, c_ref, d_ref,
+              s_ref, b4_ref, w_ref, y_ref, down_ref, up_ref, z_ref, r_ref, ride_ref, out_ref):
+    gx, gz = lax.axis_index("gx"), lax.axis_index("gz")
+    nx, nz = lax.axis_size("gx"), lax.axis_size("gz")
+
+    def margin(dz):
+        def ride(dx):
+            x, z = gx + dx, gz + dz
+            inside = (x >= 0) & (x < nx) & (z >= 0) & (z < nz)
+            at = jnp.where(inside, x * nz + z, 0)
+            return jnp.where(inside, e_ref[at, 2], 0.0)
+
+        return meet(ride(-1), ride(1))
+
+    margins = [margin(0), margin(1), margin(-1)]
+
+    def plane(z):
+        if 0 <= z < 8:
+            return square(w_ref[z], y_ref[z], margins[0], margins[0], z)
+        ref, i, at, m = (up_ref, z - 8, z - 8, 1) if z >= 8 else (down_ref, z + 4, z + 8, 2)
+        return square(ref[2 * i], ref[2 * i + 1], margins[m], margins[m], at)
+
     t = state_ref[0]
     vrow = jnp.concatenate([state_ref[1][0:1, :], state_ref[2][0:1, :]], axis=1)
     crow, grow = wide(t, 0), wide(t, 2)
@@ -398,9 +536,9 @@
     step = inner / curve
     c1 = crow - step * (grow + ev)
     v1 = solve(cinv_ref, c1)
-    r1 = {z: b4_ref[z % 16] - step * plane_of(own_ref, up_ref, down_ref, z) for z in range(-4, 12)}
+    r1 = {z: b4_ref[z % 16] - step * plane(z) for z in range(-4, 12)}
     s1 = smooth(c_ref, r1)
-    z1 = prolong(bt_ref, (fxl, fxr, fym, fyp, fzm, fzp), owner_rows(owners_ref), v1)
+    z1 = prolong(bt_ref, (lx, rx, yb, ya, zb, za), owner_rows(owners_ref), v1)
     z1 = {z: z1[z] + s1[z] for z in range(-1, 9)}
     w1 = operate(c_ref, d_ref, z1)
     zero = jnp.zeros((8, 128), F32)
@@ -413,6 +551,7 @@
         r_ref[z] = r2
         for i, (a, b) in enumerate(((r1o, s0o), (r1o, s1o), (r2, s0o), (r2, s1o))):
             sums[i] = sums[i] + a * b
+    ride_ref[0] = pack([r_ref[z] for z in range(8)])
     sub, lane = iota((8, 128), 0), iota((8, 128), 1)
     tile = zero
     for i in range(4):
@@ -426,8 +565,39 @@
     out_ref[1] = tile
 
 
-def last_body(part_ref, owners_ref, bt_ref, c_ref, d_ref, own_ref, up_ref, down_ref, s_ref, msg_ref):
-    r2 = {z: plane_of(own_ref, up_ref, down_ref, z) for z in range(-4, 12)}
+def beside_next_body(left_ref, right_ref, r_ref, m_ref, up_ref, down_ref):
+    r = [r_ref[z] for z in range(8)]
+    m = meet(left_ref[0], right_ref[0])
+    m_ref[0] = m
+    for i, (u, d) in enumerate(zip(upper(r), lower(r))):
+        up_ref[i] = u
+        down_ref[i] = d
+    up_ref[4] = m
+    down_ref[4] = m
+
+
+def beyond_next_body(below_ref, above_ref, r_ref, m_ref, y_ref, mb_ref, up_ref, down_ref):
+    y = beyond_y([above_ref[i] for i in range(4)], [below_ref[i] for i in range(4)])
+    for z in range(8):
+        y_ref[z] = y[z]
+    for i in range(4):
+        up_ref[2 * i], up_ref[2 * i + 1] = r_ref[4 + i], y[4 + i]
+        down_ref[2 * i], down_ref[2 * i + 1] = r_ref[i], y[i]
+    m = both(m_ref[0], jnp.where(iota((8, 128), 0) < 4, above_ref[4], below_ref[4]))
+    mb_ref[0] = m
+    up_ref[8] = m
+    down_ref[8] = m
+
+
+def last_body(part_ref, owners_ref, bt_ref, c_ref, d_ref, r_ref, y_ref, mb_ref, down_ref, up_ref, s_ref,
+              msg_ref):
+    def plane(z):
+        if 0 <= z < 8:
+            return square(r_ref[z], y_ref[z], mb_ref[0], mb_ref[0], z)
+        ref, i, at = (up_ref, z - 8, z - 8) if z >= 8 else (down_ref, z + 4, z + 8)
+        return square(ref[2 * i], ref[2 * i + 1], ref[8], ref[8], at)
+
+    r2 = {z: plane(z) for z in range(-4, 12)}
     s2 = smooth(c_ref, r2)
     a = operate(c_ref, d_ref, s2)
     rs = jnp.zeros((8, 128), F32)
@@ -517,83 +687,56 @@
     return below, above
 
 
-def tiles(a):
-    return a.reshape((-1, 8, 128))
-
-
 def on_device(
     right_side, perm_class, class_perm, class_store, coarse_basis, brick_owner, coarse_inverse
 ):
     group = lax.axis_size("gx") * lax.axis_size("gz")
     rows = lax.axis_size("gy")
-    owner = brick_owner.reshape(()).astype(F32)
-    owner_tile = jnp.full((1, 8, 128), owner)
-    fields, bt, fx = call(
-        first_body, [(5, 8, 8, 128), (64, BASIS, 128), (BASIS, 128)],
-        [class_perm, class_store, right_side, perm_class, coarse_basis], smem=(0, 1))
-    low = lax.broadcasted_iota(jnp.int32, (8, 128), 1) < 64
-    half = lax.broadcasted_iota(jnp.int32, (8, 128), 0) < 4
-    msg = jnp.concatenate([tiles(fields[:3]), tiles(fx), owner_tile])
-    left, right = pair(msg, msg, "gx")
-    beside = jnp.where(low, right[:24], left[:24]).reshape(3, 1, 8, 8, 128)
-    fxl, fxr = left[24:28].reshape(BASIS, 128), right[24:28].reshape(BASIS, 128)
-    ox = (left[28, :1], right[28, :1])
-    bt4 = bt.reshape(8, 8, BASIS, 128)
-    y_own = jnp.concatenate([jnp.stack(
-        [fields[0], fields[1], fields[3]])[:, None], beside], axis=1)
-    flat = tiles(y_own)
-    below, above = pair(
-        jnp.concatenate([flat, tiles(bt4[:, 7]), owner_tile]),
-        jnp.concatenate([flat, tiles(bt4[:, 0]), owner_tile]), "gy")
-    n = flat.shape[0]
-    beyond = jnp.where(half, above[:n], below[:n]).reshape(3, 2, 8, 1, 8, 128)
-    fym, fyp = below[n:n + 32].reshape(8, BASIS, 128), above[n:n + 32].reshape(8, BASIS, 128)
-    oy = (below[n + 32, :1], above[n + 32, :1])
-    own_z = jnp.concatenate([jnp.stack([fields[0], fields[1], fields[4]])[:, None], beside], axis=1)
-    own_z = jnp.concatenate([own_z[:, :, :, None], beyond], axis=3)
-    up_msg = jnp.concatenate([tiles(own_z[:, :, 4:]), tiles(bt[56:]), owner_tile])
-    down_msg = jnp.concatenate([tiles(own_z[:, :, :4]), tiles(bt[:8]), owner_tile])
-    below, above = pair(up_msg, down_msg, "gz")
-    own_c = jnp.concatenate([jnp.stack([fields[0], fields[1], fields[2]])[:, None], beside], axis=1)
-    own_c = jnp.concatenate([own_c[:, :, :, None], beyond], axis=3)
-    n = 3 * 2 * 4 * 2
-    z_down, z_up = [a[:n].reshape(3, 2, 4, 2, 8, 128) for a in (below, above)]
-    fzm, fzp = [a[n:n + 32].reshape(8, BASIS, 128) for a in (below, above)]
-    oz = (below[n + 32, :1], above[n + 32, :1])
-    owners = jnp.concatenate([owner_tile[0, :1], *ox, *oy, *oz, owner_tile[0, :1]])
-    faces = (fxl, fxr, fym, fyp, fzm, fzp)
-    ext = (16, 16, 256)
-    brick = (8, 8, 128)
-    coef, diag, s0, b4, msg = call(
-        setup_body, [(7,) + ext, brick, (10, 16, 256), ext, (group, 8, 128)],
-        [own_c, z_up, z_down, owners, bt, fx, *faces],
-        scratch=[(ext, F32), ((3,) + ext, F32)] + [((BASIS, 8192), jnp.bfloat16)] * 3)
+    tiles = lambda n: (n, 8, 128)
+    brick, ext = tiles(8), (16, 16, 256)
+    ins = [class_perm, class_store, right_side, perm_class, coarse_basis, brick_owner.reshape(1)]
+    fields, bt, mine = call(
+        first_body, [(5, 8, 8, 128), (64, BASIS, 128), tiles(8)], ins, hbm=True,
+        scratch=[pltpu.SMEM((16,), F32), pltpu.SMEM((16,), F32), pltpu.VMEM(brick, F32),
+                 pltpu.VMEM(brick, jnp.int32), pltpu.VMEM((BASIS, 8, 8, 128), jnp.bfloat16),
+                 pltpu.SMEM((1,), jnp.int32), pltpu.SemaphoreType.DMA((6,))])
+    left, right = pair(mine, mine, "gx")
+    m, up, down = call(
+        beside_body, [tiles(3), tiles(48), tiles(48)], [left, right, mine, fields, bt])
+    y_below, y_above = pair(up, down, "gy")
+    y, mb, up, down = call(
+        beyond_body, [(3, 8, 8, 128), tiles(3), tiles(63), tiles(63)],
+        [y_below, y_above, mine, fields, bt, m])
+    z_below, z_above = pair(up, down, "gz")
+    faces = (left, right, y_below, y_above, z_below, z_above)
+    coef, diag, s0, b4, msg, owners = call(
+        setup_body, [(7,) + ext, brick, (10, 16, 256), ext, (group, 8, 128), (8, 128)],
+        [fields, y, mb, z_below, z_above, left, right, y_below, y_above, mine, bt], vmem=16,
+        scratch=[pltpu.VMEM(ext, F32), pltpu.VMEM((3,) + ext, F32)]
+        + [pltpu.VMEM((BASIS, 8192), jnp.bfloat16)] * 3)
     got = lax.all_to_all(msg, PLANE, 0, 0)
-    msg, _ = call(gather_body, [(rows, 3, 8, 128), (group, 128)], [got])
+    msg = call(gather_body, (rows, 3, 8, 128), [got])
     got = lax.all_to_all(msg, "gy", 0, 0)
-    z0, w0, msg, state = call(
-        begin_body, [brick, brick, (group, 3, 8, 128), (3, 8, 128)],
+    z0, w0, up, down, e_mine, state = call(
+        begin_body, [brick, brick, tiles(4), tiles(4), tiles(2), tiles(3)],
         [got, coarse_inverse, owners, bt, *faces, coef, diag, s0])
+    below, above = pair(up, down, "gy")
+    y, up, down, msg = call(
+        ride_body, [brick, tiles(8), tiles(8), (group, 3, 8, 128)], [below, above, w0, e_mine])
     e_all = lax.all_to_all(msg, PLANE, 0, 0)
-    gx, gz = lax.axis_index("gx"), lax.axis_index("gz")
-    nz = lax.axis_size("gz")
-    at = jnp.stack([gx, (gx - 1) * nz + gz, (gx + 1) * nz + gz, jnp.int32(lax.axis_size("gx"))])
-    w_x = call(ride_body, (2, 8, 8, 128), [at.astype(jnp.int32), e_all, w0], smem=(0,))
-
-    def rest(f_x):
-        below, above = pair(f_x, f_x, "gy")
-        own = jnp.stack([f_x, jnp.where(half, above, below)], axis=2)
-        below, above = pair(own[:, 4:], own[:, :4], "gz")
-        return own, above, below
-
-    z1, r2, out1 = call(
-        next_body, [brick, brick, (2, 8, 128)],
-        [state, e_all, coarse_inverse, owners, bt, *faces, coef, diag, s0, b4, *rest(w_x)])
-    left, right = pair(r2, r2, "gx")
-    r_x = jnp.stack([r2, jnp.where(low, right, left)])
+    below, above = pair(up, down, "gz")
+    z1, r2, ride, out1 = call(
+        next_body, [brick, brick, tiles(1), tiles(2)],
+        [state, e_all, coarse_inverse, owners, bt, *faces, coef, diag, s0, b4, w0, y, below, above])
+    left, right = pair(ride, ride, "gx")
+    m, up, down = call(beside_next_body, [tiles(1), tiles(5), tiles(5)], [left, right, r2])
+    below, above = pair(up, down, "gy")
+    y, mb, up, down = call(
+        beyond_next_body, [brick, tiles(1), tiles(9), tiles(9)], [below, above, r2, m])
+    below, above = pair(up, down, "gz")
     s2, msg = call(
         last_body, [brick, (group, 8, 128)],
-        [out1, owners, bt, coef, diag, *rest(r_x)])
+        [out1, owners, bt, coef, diag, r2, y, mb, below, above])
     got = lax.all_to_all(msg, PLANE, 0, 0)
     msg = call(gather_last_body, (rows, 8, 128), [got])
     got = lax.all_to_all(msg, "gy", 0, 0)

time: 192 us -> 184 us (0.958)
  blocking collectives: 80.3 us -> 74.7 us
  local copies, waits for them, and re-layouts: 12.2 us -> 17.7 us
  starting transfers between devices: 61.4 us -> 56.1 us
  other arithmetic: 2.6 us -> 0 us
    ppermute x8, waiting for transfers between devices: 2.86 us -> 21.3 us  [pair(): above = lax.ppermute(down_part, axis, down)]
    ppermute x8, starting transfers between devices: 23.2 us -> 13.4 us  [pair(): above = lax.ppermute(down_part, axis, down)]
    all_to_all x1, waiting for transfers between devices: 9.61 us -> 0.47 us  [on_device(): e_all = lax.all_to_all(msg, PLANE, 0, 0)]
    ppermute x8, waiting for transfers between devices: 12.1 us -> 3.21 us  [pair(): below = lax.ppermute(up_part, axis, up)]
    ppermute x8, starting transfers between devices: 30.8 us -> 36.7 us  [pair(): below = lax.ppermute(up_part, axis, up)]
    all_to_all x2, blocking collectives: 51.4 us -> 45.6 us  [on_device(): got = lax.all_to_all(msg, 'gy', 0, 0)]
    unnamed x74 -> x64, local copies, waits for them, and re-layouts: 12 us -> 17.7 us
    pallas_call x9 -> x13, Pallas kernels: 8.49 us -> 8.19 us  [call(): pl.pallas_call(body, out_shape=shapes, in_specs=[pl.BlockSpec(memory_spac...]
  transfers between devices with their start and end apart: 17 -> 17, of which waited for: 12 -> 11; matrix products, arithmetic and copies ran while one was open for 1% -> 0% of each run, Pallas kernels for 0% -> 0%
where the time goes in v2:
time: 184 us; the launch traced here: 183 us
  blocking collectives  74.7 us (41%)
  starting transfers between devices  56.1 us (30%)
  waiting for transfers between devices  25 us (14%)
  local copies, waits for them, and re-layouts  17.7 us (10%)
  Pallas kernels  8.19 us (4%)
    all_to_all x2, blocking collectives, on_device(): got = lax.all_to_all(msg, 'gy', 0, 0)  45.6 us
    ppermute x8, starting transfers between devices, pair(): below = lax.ppermute(up_part, axis, up)  36.7 us
    all_to_all x2, blocking collectives, on_device(): got = lax.all_to_all(msg, PLANE, 0, 0)  29.1 us
    ppermute x8, waiting for transfers between devices, pair(): above = lax.ppermute(down_part, axis, down)  21.3 us
    unnamed x64, local copies, waits for them, and re-layouts  17.7 us
    ppermute x8, starting transfers between devices, pair(): above = lax.ppermute(down_part, axis, down)  13.4 us
    pallas_call x13, Pallas kernels, call(): pl.pallas_call(body, out_shape=shapes, in_specs=[pl.BlockSpec(memory_spac...  8.19 us
    all_to_all x1, starting transfers between devices, on_device(): e_all = lax.all_to_all(msg, PLANE, 0, 0)  6.03 us
  transfers between devices with their start and end apart: 17, of which 11 were waited for; matrix products, arithmetic and copies ran while one was open for 0% of the time, Pallas kernels for 0%

profile of v2, /device:TPU:1, one launch (start us, length us, event | category | flops | bytes accessed | tf_op | source)
XLA Modules:
  0.0 182.7 jit_solution(4059607550144503475)
XLA Ops:
  0.7 1.0 copy-done.10
  1.7 0.8 copy-done.26
  2.5 0.8 copy-done.27
  3.2 0.7 copy-done.28
  3.9 0.7 copy-done.29
  4.5 1.3 shard_map.73
  5.9 1.3 collective-permute-start.1
  7.2 4.7 %collective-permute-start = (f32[8,8,128]{2,1,0:T(8,128)S(1)}, f32[8,8,128]{2,1,0:T(8,128)S(1)}, u32[]{:S(2)}, u32[]{:S(2)}) collective-permute-start(f32[8,8,128]{2,1,0:T(8,128)S(1)} %get-tuple-element.45.mine_ref), channel_id=1, source_target_pairs={{0,128},{128,256},{256,384},{1,129},{129,257},{257,385},{2,130},{1... | collective-permute-start | bytes 98312 | tf_op jit(solution)/shard_map/ppermute | solution.py:685
  11.8 1.0 collective-permute-done.left_ref.lx_ref.lx
  12.9 3.7 %collective-permute-start.2 = (f32[48,8,128]{2,1,0:T(8,128)S(1)}, f32[48,8,128]{2,1,0:T(8,128)S(1)}, u32[]{:S(2)}, u32[]{:S(2)}) collective-permute-start(f32[48,8,128]{2,1,0:T(8,128)S(1)} %get-tuple-element.47), channel_id=1, source_target_pairs={{0,8},{8,16},{16,24},{24,32},{32,40},{40,48},{48,56},{56,64},{64,7... | collective-permute-start | bytes 589832 | tf_op jit(solution)/shard_map/ppermute | solution.py:685
  16.6 1.3 collective-permute-start.3
  17.9 1.3 collective-permute-done.2.below_ref.yb_ref.yb
  19.2 4.0 %collective-permute-done.3.above_ref.ya_ref.ya = f32[48,8,128]{2,1,0:T(8,128)S(1)} collective-permute-done((f32[48,8,128]{2,1,0:T(8,128)S(1)}, f32[48,8,128]{2,1,0:T(8,128)S(1)}, u32[]{:S(2)}, u32[]{:S(2)}) %collective-permute-start.3) | collective-permute-done | bytes 196640 | tf_op jit(solution)/shard_map/ppermute | solution.py:686
  23.2 0.1 shard_map.75
  23.3 6.2 %collective-permute-start.4 = (f32[63,8,128]{2,1,0:T(8,128)S(1)}, f32[63,8,128]{2,1,0:T(8,128)S(1)}, u32[]{:S(2)}, u32[]{:S(2)}) collective-permute-start(f32[63,8,128]{2,1,0:T(8,128)S(1)} %get-tuple-element.52), channel_id=1, source_target_pairs={{0,1},{1,2},{2,3},{3,4},{4,5},{5,6},{6,7},{8,9},{9,10},{10,11},{11... | collective-permute-start | bytes 774152 | tf_op jit(solution)/shard_map/ppermute | solution.py:685
  29.5 3.1 %collective-permute-start.5 = (f32[63,8,128]{2,1,0:T(8,128)S(1)}, f32[63,8,128]{2,1,0:T(8,128)S(1)}, u32[]{:S(2)}, u32[]{:S(2)}) collective-permute-start(f32[63,8,128]{2,1,0:T(8,128)S(1)} %get-tuple-element.53), channel_id=1, source_target_pairs={{1,0},{2,1},{3,2},{4,3},{5,4},{6,5},{7,6},{9,8},{10,9},{11,10},{12... | collective-permute-start | bytes 774152 | tf_op jit(solution)/shard_map/ppermute | solution.py:686
  32.5 0.2 collective-permute-done.4.zb_ref.zb
  32.7 4.4 %collective-permute-done.5.za_ref.za = f32[63,8,128]{2,1,0:T(8,128)S(1)} collective-permute-done((f32[63,8,128]{2,1,0:T(8,128)S(1)}, f32[63,8,128]{2,1,0:T(8,128)S(1)}, u32[]{:S(2)}, u32[]{:S(2)}) %collective-permute-start.5) | collective-permute-done | bytes 258080 | tf_op jit(solution)/shard_map/ppermute | solution.py:686
  37.1 2.6 %shard_map.76 = (f32[7,16,16,256]{3,2,1,0:T(8,128)S(1)}, f32[8,8,128]{2,1,0:T(8,128)S(1)}, f32[10,16,256]{2,1,0:T(8,128)S(1)}, f32[16,16,256]{2,1,0:T(8,128)S(1)...) custom-call(f32[5,8,8,128]{3,2,1,0:T(8,128)S(1)} %get-tuple-element.44.f_ref, ...), custom_call_target="tpu_custom_call" | custom-call | tf_op jit(solution)/shard_map/pallas_call | solution.py:22
  39.8 15.2 %all_to_all.25.got_ref = f32[32,8,128]{2,1,0:T(8,128)S(1)} all-to-all(f32[32,8,128]{2,1,0:T(8,128)S(1)} %get-tuple-element.54), channel_id=1, replica_groups=mesh['gx'=4,'gy'=16,'gz'=8] {'gx','gz'}, dimensions={0} | all-to-all | bytes 262144 | tf_op jit(solution)/shard_map/all_to_all | solution.py:717
  54.9 0.1 shard_map.77
  55.0 27.4 %all_to_all.26.got_ref = f32[16,3,8,128]{3,2,1,0:T(8,128)S(1)} all-to-all(f32[16,3,8,128]{3,2,1,0:T(8,128)S(1)} %shard_map.77), channel_id=1, replica_groups=mesh['gx'=4,'gy'=16,'gz'=8] {'gy'}, dimensions={0} | all-to-all | bytes 393216 | tf_op jit(solution)/shard_map/all_to_all | solution.py:719
  82.4 0.5 shard_map.78
  83.0 0.6 copy-done.18
  83.6 6.5 %collective-permute-start.6 = (f32[4,8,128]{2,1,0:T(8,128)S(1)}, f32[4,8,128]{2,1,0:T(8,128)S(1)}, u32[]{:S(2)}, u32[]{:S(2)}) collective-permute-start(f32[4,8,128]{2,1,0:T(8,128)S(1)} %get-tuple-element.60), channel_id=1, source_target_pairs={{0,8},{8,16},{16,24},{24,32},{32,40},{40,48},{48,56},{56,64},{64,7... | collective-permute-start | bytes 49160 | tf_op jit(solution)/shard_map/ppermute | solution.py:685
  90.1 1.3 collective-permute-start.7
  91.4 3.2 %collective-permute-done.7.above_ref = f32[4,8,128]{2,1,0:T(8,128)S(1)} collective-permute-done((f32[4,8,128]{2,1,0:T(8,128)S(1)}, f32[4,8,128]{2,1,0:T(8,128)S(1)}, u32[]{:S(2)}, u32[]{:S(2)}) %collective-permute-start.7) | collective-permute-done | bytes 16416 | tf_op jit(solution)/shard_map/ppermute | solution.py:686
  94.6 0.1 shard_map.79
  94.7 0.7 copy-done.11
  95.5 0.6 copy-done.20
  96.1 0.6 copy-done.30
  96.7 0.6 copy-done.31
  97.3 6.0 %all-to-all-start.2 = ((f32[32,3,8,128]{3,2,1,0:T(8,128)}), f32[32,3,8,128]{3,2,1,0:T(8,128)S(1)}, u32[]{:S(2)}, u32[]{:S(2)}) async-start(f32[32,3,8,128]{3,2,1,0:T(8,128)} %copy-done.11), calls=%async_computation.2 | async-start | bytes 786432 | tf_op jit(solution)/shard_map/all_to_all | solution.py:726
  103.3 3.5 %collective-permute-start.8 = (f32[8,8,128]{2,1,0:T(8,128)}, f32[8,8,128]{2,1,0:T(8,128)S(1)}, u32[]{:S(2)}, u32[]{:S(2)}) collective-permute-start(f32[8,8,128]{2,1,0:T(8,128)} %copy-done.31), channel_id=1, source_target_pairs={{0,1},{1,2},{2,3},{3,4},{4,5},{5,6},{6,7},{8,9},{9,10},{10,11},{11... | collective-permute-start | bytes 98312 | tf_op jit(solution)/shard_map/ppermute | solution.py:685
  106.9 1.9 %collective-permute-start.9 = (f32[8,8,128]{2,1,0:T(8,128)}, f32[8,8,128]{2,1,0:T(8,128)S(1)}, u32[]{:S(2)}, u32[]{:S(2)}) collective-permute-start(f32[8,8,128]{2,1,0:T(8,128)} %copy-done.30), channel_id=1, source_target_pairs={{1,0},{2,1},{3,2},{4,3},{5,4},{6,5},{7,6},{9,8},{10,9},{11,10},{12... | collective-permute-start | bytes 98312 | tf_op jit(solution)/shard_map/ppermute | solution.py:686
  108.8 0.6 copy-done.22
  109.4 3.2 %collective-permute-done.9.up_ref = f32[8,8,128]{2,1,0:T(8,128)S(1)} collective-permute-done((f32[8,8,128]{2,1,0:T(8,128)}, f32[8,8,128]{2,1,0:T(8,128)S(1)}, u32[]{:S(2)}, u32[]{:S(2)}) %collective-permute-start.9) | collective-permute-done | bytes 32800 | tf_op jit(solution)/shard_map/ppermute | solution.py:686
  112.6 0.6 copy-done.24
  113.2 0.5 all-to-all-done.2.e_ref
  113.7 0.9 copy-done.1
  114.6 0.9 copy-done.3
  115.5 0.9 copy-done.5
  116.5 0.9 copy-done.7
  117.4 0.9 copy-done.9
  118.4 0.8 copy-done.13
  119.1 0.9 copy-done.15
  120.1 0.8 copy-done.17
  120.8 0.8 copy-done.21
  121.6 0.8 copy-done.23
  122.3 0.8 copy-done.25
  123.1 1.1 shard_map.80
  124.2 1.3 collective-permute-start.11
  125.6 4.0 %collective-permute-start.10 = (f32[1,8,128]{2,1,0:T(8,128)S(1)}, f32[1,8,128]{2,1,0:T(8,128)S(1)}, u32[]{:S(2)}, u32[]{:S(2)}) collective-permute-start(f32[1,8,128]{2,1,0:T(8,128)S(1)} %get-tuple-element.71), channel_id=1, source_target_pairs={{0,128},{128,256},{256,384},{1,129},{129,257},{257,385},{2,130},{1... | collective-permute-start | bytes 12296 | tf_op jit(solution)/shard_map/ppermute | solution.py:685
  129.6 0.7 collective-permute-done.10.left_ref
  130.3 3.2 %collective-permute-start.12 = (f32[5,8,128]{2,1,0:T(8,128)S(1)}, f32[5,8,128]{2,1,0:T(8,128)S(1)}, u32[]{:S(2)}, u32[]{:S(2)}) collective-permute-start(f32[5,8,128]{2,1,0:T(8,128)S(1)} %get-tuple-element.72), channel_id=1, source_target_pairs={{0,8},{8,16},{16,24},{24,32},{32,40},{40,48},{48,56},{56,64},{64,7... | collective-permute-start | bytes 61448 | tf_op jit(solution)/shard_map/ppermute | solution.py:685
  133.5 1.3 collective-permute-start.13
  134.8 3.2 %collective-permute-done.13.above_ref = f32[5,8,128]{2,1,0:T(8,128)S(1)} collective-permute-done((f32[5,8,128]{2,1,0:T(8,128)S(1)}, f32[5,8,128]{2,1,0:T(8,128)S(1)}, u32[]{:S(2)}, u32[]{:S(2)}) %collective-permute-start.13) | collective-permute-done | bytes 20512 | tf_op jit(solution)/shard_map/ppermute | solution.py:686
  138.1 4.9 %collective-permute-start.14 = (f32[9,8,128]{2,1,0:T(8,128)S(1)}, f32[9,8,128]{2,1,0:T(8,128)S(1)}, u32[]{:S(2)}, u32[]{:S(2)}) collective-permute-start(f32[9,8,128]{2,1,0:T(8,128)S(1)} %get-tuple-element.77), channel_id=1, source_target_pairs={{0,1},{1,2},{2,3},{3,4},{4,5},{5,6},{6,7},{8,9},{9,10},{10,11},{11... | collective-permute-start | bytes 110600 | tf_op jit(solution)/shard_map/ppermute | solution.py:685
  143.1 1.9 %collective-permute-start.15 = (f32[9,8,128]{2,1,0:T(8,128)S(1)}, f32[9,8,128]{2,1,0:T(8,128)S(1)}, u32[]{:S(2)}, u32[]{:S(2)}) collective-permute-start(f32[9,8,128]{2,1,0:T(8,128)S(1)} %get-tuple-element.78), channel_id=1, source_target_pairs={{1,0},{2,1},{3,2},{4,3},{5,4},{6,5},{7,6},{9,8},{10,9},{11,10},{12... | collective-permute-start | bytes 110600 | tf_op jit(solution)/shard_map/ppermute | solution.py:686
  145.0 3.3 %collective-permute-done.15.up_ref = f32[9,8,128]{2,1,0:T(8,128)S(1)} collective-permute-done((f32[9,8,128]{2,1,0:T(8,128)S(1)}, f32[9,8,128]{2,1,0:T(8,128)S(1)}, u32[]{:S(2)}, u32[]{:S(2)}) %collective-permute-start.15) | collective-permute-done | bytes 36896 | tf_op jit(solution)/shard_map/ppermute | solution.py:686
  148.3 0.8 shard_map.83
  149.2 13.9 %all_to_all.27.got_ref = f32[32,8,128]{2,1,0:T(8,128)S(1)} all-to-all(f32[32,8,128]{2,1,0:T(8,128)S(1)} %get-tuple-element.79), channel_id=1, replica_groups=mesh['gx'=4,'gy'=16,'gz'=8] {'gx','gz'}, dimensions={0} | all-to-all | bytes 262144 | tf_op jit(solution)/shard_map/all_to_all | solution.py:740
  163.1 18.2 %all_to_all.28.got_ref = f32[16,8,128]{2,1,0:T(8,128)S(1)} all-to-all(f32[16,8,128]{2,1,0:T(8,128)S(1)} %shard_map.84), channel_id=1, replica_groups=mesh['gx'=4,'gy'=16,'gz'=8] {'gy'}, dimensions={0} | all-to-all | bytes 131072 | tf_op jit(solution)/shard_map/all_to_all | solution.py:742
  181.3 1.4 shard_map.85
  (51 shorter events, 0.3 us)
Async XLA Ops:
  0.7 1.0 copy-start.10
  1.7 0.8 copy-start.26
  2.5 0.8 copy-start.27
  3.2 0.7 copy-start.28
  3.9 0.7 copy-start.29
  5.9 6.0 %collective-permute-start.1 = (f32[8,8,128]{2,1,0:T(8,128)S(1)}, f32[8,8,128]{2,1,0:T(8,128)S(1)}, u32[]{:S(2)}, u32[]{:S(2)}) collective-permute-start(f32[8,8,128]{2,1,0:T(8,128)S(1)} %get-tuple-element.45.mine_ref), channel_id=1, source_target_pairs={{128,0},{256,128},{384,256},{129,1},{257,129},{385,257},{130,2},{2... | collective-permute-start | bytes 98312 | tf_op jit(solution)/shard_map/ppermute | solution.py:686
  7.2 5.7 %collective-permute-start = (f32[8,8,128]{2,1,0:T(8,128)S(1)}, f32[8,8,128]{2,1,0:T(8,128)S(1)}, u32[]{:S(2)}, u32[]{:S(2)}) collective-permute-start(f32[8,8,128]{2,1,0:T(8,128)S(1)} %get-tuple-element.45.mine_ref), channel_id=1, source_target_pairs={{0,128},{128,256},{256,384},{1,129},{129,257},{257,385},{2,130},{1... | collective-permute-start | bytes 98312 | tf_op jit(solution)/shard_map/ppermute | solution.py:685
  12.9 6.3 %collective-permute-start.2 = (f32[48,8,128]{2,1,0:T(8,128)S(1)}, f32[48,8,128]{2,1,0:T(8,128)S(1)}, u32[]{:S(2)}, u32[]{:S(2)}) collective-permute-start(f32[48,8,128]{2,1,0:T(8,128)S(1)} %get-tuple-element.47), channel_id=1, source_target_pairs={{0,8},{8,16},{16,24},{24,32},{32,40},{40,48},{48,56},{56,64},{64,7... | collective-permute-start | bytes 589832 | tf_op jit(solution)/shard_map/ppermute | solution.py:685
  16.6 6.6 %collective-permute-start.3 = (f32[48,8,128]{2,1,0:T(8,128)S(1)}, f32[48,8,128]{2,1,0:T(8,128)S(1)}, u32[]{:S(2)}, u32[]{:S(2)}) collective-permute-start(f32[48,8,128]{2,1,0:T(8,128)S(1)} %get-tuple-element.48), channel_id=1, source_target_pairs={{8,0},{16,8},{24,16},{32,24},{40,32},{48,40},{56,48},{64,56},{72,6... | collective-permute-start | bytes 589832 | tf_op jit(solution)/shard_map/ppermute | solution.py:686
  23.2 59.2 %copy-start = (f32[48,8,128]{2,1,0:T(8,128)}, f32[48,8,128]{2,1,0:T(8,128)S(1)}, u32[]{:S(2)}) copy-start(f32[48,8,128]{2,1,0:T(8,128)S(1)} %collective-permute-done.3.above_ref.ya_ref.ya) | copy-start | bytes 589828
  23.3 59.1 %copy-start.2 = (f32[256,256]{1,0:T(8,128)S(1)}, f32[256,256]{1,0:T(8,128)}, u32[]{:S(2)}) copy-start(f32[256,256]{1,0:T(8,128)} %cinv_ref.5) | copy-start | bytes 786436
  23.3 9.4 %collective-permute-start.4 = (f32[63,8,128]{2,1,0:T(8,128)S(1)}, f32[63,8,128]{2,1,0:T(8,128)S(1)}, u32[]{:S(2)}, u32[]{:S(2)}) collective-permute-start(f32[63,8,128]{2,1,0:T(8,128)S(1)} %get-tuple-element.52), channel_id=1, source_target_pairs={{0,1},{1,2},{2,3},{3,4},{4,5},{5,6},{6,7},{8,9},{9,10},{10,11},{11... | collective-permute-start | bytes 774152 | tf_op jit(solution)/shard_map/ppermute | solution.py:685
  29.5 7.6 %collective-permute-start.5 = (f32[63,8,128]{2,1,0:T(8,128)S(1)}, f32[63,8,128]{2,1,0:T(8,128)S(1)}, u32[]{:S(2)}, u32[]{:S(2)}) collective-permute-start(f32[63,8,128]{2,1,0:T(8,128)S(1)} %get-tuple-element.53), channel_id=1, source_target_pairs={{1,0},{2,1},{3,2},{4,3},{5,4},{6,5},{7,6},{9,8},{10,9},{11,10},{12... | collective-permute-start | bytes 774152 | tf_op jit(solution)/shard_map/ppermute | solution.py:686
  32.7 50.2 %copy-start.4 = (f32[63,8,128]{2,1,0:T(8,128)}, f32[63,8,128]{2,1,0:T(8,128)S(1)}, u32[]{:S(2)}) copy-start(f32[63,8,128]{2,1,0:T(8,128)S(1)} %collective-permute-done.4.zb_ref.zb) | copy-start | bytes 774148
  37.1 45.8 %copy-start.6 = (f32[63,8,128]{2,1,0:T(8,128)}, f32[63,8,128]{2,1,0:T(8,128)S(1)}, u32[]{:S(2)}) copy-start(f32[63,8,128]{2,1,0:T(8,128)S(1)} %collective-permute-done.5.za_ref.za) | copy-start | bytes 774148
  39.7 43.2 %copy-start.8 = (f32[10,16,256]{2,1,0:T(8,128)}, f32[10,16,256]{2,1,0:T(8,128)S(1)}, u32[]{:S(2)}) copy-start(f32[10,16,256]{2,1,0:T(8,128)S(1)} %get-tuple-element.58.s_ref) | copy-start | bytes 491524
  39.7 43.2 %copy-start.12 = (f32[8,8,128]{2,1,0:T(8,128)}, f32[8,8,128]{2,1,0:T(8,128)S(1)}, u32[]{:S(2)}) copy-start(f32[8,8,128]{2,1,0:T(8,128)S(1)} %get-tuple-element.57.d_ref) | copy-start | bytes 98308
  39.7 43.2 %copy-start.14 = (f32[16,16,256]{2,1,0:T(8,128)}, f32[16,16,256]{2,1,0:T(8,128)S(1)}, u32[]{:S(2)}) copy-start(f32[16,16,256]{2,1,0:T(8,128)S(1)} %get-tuple-element.65.b4_ref) | copy-start | bytes 786436
  83.0 0.6 copy-start.18
  83.6 11.1 %copy-start.16 = (f32[8,8,128]{2,1,0:T(8,128)}, f32[8,8,128]{2,1,0:T(8,128)S(1)}, u32[]{:S(2)}) copy-start(f32[8,8,128]{2,1,0:T(8,128)S(1)} %get-tuple-element.62.w_ref) | copy-start | bytes 98308
  83.6 7.8 %collective-permute-start.6 = (f32[4,8,128]{2,1,0:T(8,128)S(1)}, f32[4,8,128]{2,1,0:T(8,128)S(1)}, u32[]{:S(2)}, u32[]{:S(2)}) collective-permute-start(f32[4,8,128]{2,1,0:T(8,128)S(1)} %get-tuple-element.60), channel_id=1, source_target_pairs={{0,8},{8,16},{16,24},{24,32},{32,40},{40,48},{48,56},{56,64},{64,7... | collective-permute-start | bytes 49160 | tf_op jit(solution)/shard_map/ppermute | solution.py:685
  90.1 4.5 %collective-permute-start.7 = (f32[4,8,128]{2,1,0:T(8,128)S(1)}, f32[4,8,128]{2,1,0:T(8,128)S(1)}, u32[]{:S(2)}, u32[]{:S(2)}) collective-permute-start(f32[4,8,128]{2,1,0:T(8,128)S(1)} %get-tuple-element.61), channel_id=1, source_target_pairs={{8,0},{16,8},{24,16},{32,24},{40,32},{48,40},{56,48},{64,56},{72,6... | collective-permute-start | bytes 49160 | tf_op jit(solution)/shard_map/ppermute | solution.py:686
  94.7 0.8 copy-start.11
  95.5 0.6 copy-start.20
  96.1 0.6 copy-start.30
  96.7 0.6 copy-start.31
  97.3 16.4 %all-to-all-start.2 = ((f32[32,3,8,128]{3,2,1,0:T(8,128)}), f32[32,3,8,128]{3,2,1,0:T(8,128)S(1)}, u32[]{:S(2)}, u32[]{:S(2)}) async-start(f32[32,3,8,128]{3,2,1,0:T(8,128)} %copy-done.11), calls=%async_computation.2 | async-start | bytes 786432 | tf_op jit(solution)/shard_map/all_to_all | solution.py:726
  103.3 5.5 %collective-permute-start.8 = (f32[8,8,128]{2,1,0:T(8,128)}, f32[8,8,128]{2,1,0:T(8,128)S(1)}, u32[]{:S(2)}, u32[]{:S(2)}) collective-permute-start(f32[8,8,128]{2,1,0:T(8,128)} %copy-done.31), channel_id=1, source_target_pairs={{0,1},{1,2},{2,3},{3,4},{4,5},{5,6},{6,7},{8,9},{9,10},{10,11},{11... | collective-permute-start | bytes 98312 | tf_op jit(solution)/shard_map/ppermute | solution.py:685
  106.9 5.7 %collective-permute-start.9 = (f32[8,8,128]{2,1,0:T(8,128)}, f32[8,8,128]{2,1,0:T(8,128)S(1)}, u32[]{:S(2)}, u32[]{:S(2)}) collective-permute-start(f32[8,8,128]{2,1,0:T(8,128)} %copy-done.30), channel_id=1, source_target_pairs={{1,0},{2,1},{3,2},{4,3},{5,4},{6,5},{7,6},{9,8},{10,9},{11,10},{12... | collective-permute-start | bytes 98312 | tf_op jit(solution)/shard_map/ppermute | solution.py:686
  108.8 0.6 copy-start.22
  112.6 0.6 copy-start.24
  113.7 0.9 copy-start.1
  114.6 0.9 copy-start.3
  115.5 0.9 copy-start.5
  116.5 0.9 copy-start.7
  117.4 0.9 copy-start.9
  118.4 0.8 copy-start.13
  119.1 0.9 copy-start.15
  120.1 0.8 copy-start.17
  120.8 0.8 copy-start.21
  121.6 0.8 copy-start.23
  122.3 0.8 copy-start.25
  124.2 5.3 %collective-permute-start.11 = (f32[1,8,128]{2,1,0:T(8,128)S(1)}, f32[1,8,128]{2,1,0:T(8,128)S(1)}, u32[]{:S(2)}, u32[]{:S(2)}) collective-permute-start(f32[1,8,128]{2,1,0:T(8,128)S(1)} %get-tuple-element.71), channel_id=1, source_target_pairs={{128,0},{256,128},{384,256},{129,1},{257,129},{385,257},{130,2},{2... | collective-permute-start | bytes 12296 | tf_op jit(solution)/shard_map/ppermute | solution.py:686
  125.6 4.7 %collective-permute-start.10 = (f32[1,8,128]{2,1,0:T(8,128)S(1)}, f32[1,8,128]{2,1,0:T(8,128)S(1)}, u32[]{:S(2)}, u32[]{:S(2)}) collective-permute-start(f32[1,8,128]{2,1,0:T(8,128)S(1)} %get-tuple-element.71), channel_id=1, source_target_pairs={{0,128},{128,256},{256,384},{1,129},{129,257},{257,385},{2,130},{1... | collective-permute-start | bytes 12296 | tf_op jit(solution)/shard_map/ppermute | solution.py:685
  130.3 4.5 %collective-permute-start.12 = (f32[5,8,128]{2,1,0:T(8,128)S(1)}, f32[5,8,128]{2,1,0:T(8,128)S(1)}, u32[]{:S(2)}, u32[]{:S(2)}) collective-permute-start(f32[5,8,128]{2,1,0:T(8,128)S(1)} %get-tuple-element.72), channel_id=1, source_target_pairs={{0,8},{8,16},{16,24},{24,32},{32,40},{40,48},{48,56},{56,64},{64,7... | collective-permute-start | bytes 61448 | tf_op jit(solution)/shard_map/ppermute | solution.py:685
  133.5 4.5 %collective-permute-start.13 = (f32[5,8,128]{2,1,0:T(8,128)S(1)}, f32[5,8,128]{2,1,0:T(8,128)S(1)}, u32[]{:S(2)}, u32[]{:S(2)}) collective-permute-start(f32[5,8,128]{2,1,0:T(8,128)S(1)} %get-tuple-element.73), channel_id=1, source_target_pairs={{8,0},{16,8},{24,16},{32,24},{40,32},{48,40},{56,48},{64,56},{72,6... | collective-permute-start | bytes 61448 | tf_op jit(solution)/shard_map/ppermute | solution.py:686
  138.1 6.9 %collective-permute-start.14 = (f32[9,8,128]{2,1,0:T(8,128)S(1)}, f32[9,8,128]{2,1,0:T(8,128)S(1)}, u32[]{:S(2)}, u32[]{:S(2)}) collective-permute-start(f32[9,8,128]{2,1,0:T(8,128)S(1)} %get-tuple-element.77), channel_id=1, source_target_pairs={{0,1},{1,2},{2,3},{3,4},{4,5},{5,6},{6,7},{8,9},{9,10},{10,11},{11... | collective-permute-start | bytes 110600 | tf_op jit(solution)/shard_map/ppermute | solution.py:685
  143.1 5.3 %collective-permute-start.15 = (f32[9,8,128]{2,1,0:T(8,128)S(1)}, f32[9,8,128]{2,1,0:T(8,128)S(1)}, u32[]{:S(2)}, u32[]{:S(2)}) collective-permute-start(f32[9,8,128]{2,1,0:T(8,128)S(1)} %get-tuple-element.78), channel_id=1, source_target_pairs={{1,0},{2,1},{3,2},{4,3},{5,4},{6,5},{7,6},{9,8},{10,9},{11,10},{12... | collective-permute-start | bytes 110600 | tf_op jit(solution)/shard_map/ppermute | solution.py:686
  148.3 33.0 %copy-start.19 = (f32[8,8,128]{2,1,0:T(8,128)S(1)}, f32[8,8,128]{2,1,0:T(8,128)}, u32[]{:S(2)}) copy-start(f32[8,8,128]{2,1,0:T(8,128)} %copy-done.18) | copy-start | bytes 98308

commit v3 on v2

--- a/solution.py
+++ b/solution.py
@@ -194,23 +194,17 @@
     return jnp.concatenate([ref[start + i] for i in range(4)], axis=0)
 
 
-def first_body(perm_hbm, store_hbm, b_hbm, cls_hbm, basis_hbm, owner_hbm, f_ref, bt_ref, msg_ref,
-               perm_ref, store_ref, b_ref, cls_ref, basis_ref, owner_ref, sems):
-    copies = [pltpu.make_async_copy(src, dst, sems.at[i]) for i, (src, dst) in enumerate((
-        (perm_hbm, perm_ref), (store_hbm, store_ref), (owner_hbm, owner_ref), (cls_hbm, cls_ref),
-        (b_hbm, b_ref), (basis_hbm, basis_ref)))]
-    for c in copies:
-        c.start()
-    for c in copies[:5]:
-        c.wait()
+def first_body(in_ref, basis_ref, f_ref, bt_ref, msg_ref):
+    b_ref = in_ref
+    table = in_ref[16]
     ks, sts = [], []
     for z in range(8):
-        c = cls_ref[z]
+        c = in_ref[8 + z]
         k = jnp.zeros((8, 128), F32)
         st = jnp.zeros((8, 128), F32)
         for i in range(16):
-            k = jnp.where(c == i, perm_ref[i], k)
-            st = jnp.where(c == i, store_ref[i], st)
+            k = jnp.where(c == i, table[0:1, i:i + 1], k)
+            st = jnp.where(c == i, table[1:2, i:i + 1], st)
         ks.append(k)
         sts.append(st)
     sub = iota((8, 128), 0)
@@ -232,8 +226,7 @@
         stx.append(sts[z] + jnp.where(
             lane8 == 3, face, jnp.where(lane8 == 124, pltpu.roll(face, 1, 1), 0.0)))
     msg_ref[2] = pack(stx)
-    msg_ref[X_OWN] = jnp.broadcast_to(owner_ref[0].astype(F32), (8, 128))
-    copies[5].wait()
+    msg_ref[X_OWN] = in_ref[17]
     lane = iota((BASIS, 128), 1)
     lo = jnp.zeros((BASIS, 128), F32)
     hi = jnp.zeros((BASIS, 128), F32)
@@ -680,10 +673,15 @@
 
 def pair(up_part, down_part, axis):
     size = lax.axis_size(axis)
-    up = [(i, i + 1) for i in range(size - 1)]
+    closed = axis == "gz"
+    up = [(i, (i + 1) % size) for i in range(size if closed else size - 1)]
     down = [(j, i) for i, j in up]
     below = lax.ppermute(up_part, axis, up)
     above = lax.ppermute(down_part, axis, down)
+    if closed:
+        at = lax.axis_index(axis)
+        below = jnp.where(at > 0, below, 0.0)
+        above = jnp.where(at < size - 1, above, 0.0)
     return below, above
 
 
@@ -694,12 +692,13 @@
     rows = lax.axis_size("gy")
     tiles = lambda n: (n, 8, 128)
     brick, ext = tiles(8), (16, 16, 256)
-    ins = [class_perm, class_store, right_side, perm_class, coarse_basis, brick_owner.reshape(1)]
+    tables = jnp.stack([class_perm, class_store])
+    tables = jnp.pad(tables, ((0, 6), (0, 128 - tables.shape[1])))
+    first = jnp.concatenate([
+        right_side, perm_class.astype(F32), tables[None],
+        jnp.broadcast_to(brick_owner.astype(F32), tiles(1))])
     fields, bt, mine = call(
-        first_body, [(5, 8, 8, 128), (64, BASIS, 128), tiles(8)], ins, hbm=True,
-        scratch=[pltpu.SMEM((16,), F32), pltpu.SMEM((16,), F32), pltpu.VMEM(brick, F32),
-                 pltpu.VMEM(brick, jnp.int32), pltpu.VMEM((BASIS, 8, 8, 128), jnp.bfloat16),
-                 pltpu.SMEM((1,), jnp.int32), pltpu.SemaphoreType.DMA((6,))])
+        first_body, [(5, 8, 8, 128), (64, BASIS, 128), tiles(8)], [first, coarse_basis])
     left, right = pair(mine, mine, "gx")
     m, up, down = call(
         beside_body, [tiles(3), tiles(48), tiles(48)], [left, right, mine, fields, bt])
@@ -723,8 +722,9 @@
     below, above = pair(up, down, "gy")
     y, up, down, msg = call(
         ride_body, [brick, tiles(8), tiles(8), (group, 3, 8, 128)], [below, above, w0, e_mine])
+    below, above = pair(up, down, "gz")
+    msg, below, above = lax.optimization_barrier((msg, below, above))
     e_all = lax.all_to_all(msg, PLANE, 0, 0)
-    below, above = pair(up, down, "gz")
     z1, r2, ride, out1 = call(
         next_body, [brick, brick, tiles(1), tiles(2)],
         [state, e_all, coarse_inverse, owners, bt, *faces, coef, diag, s0, b4, w0, y, below, above])

time: 184 us -> 169 us (0.918)
  local copies, waits for them, and re-layouts: 17.7 us -> 1.12 us
  blocking collectives: 74.7 us -> 90.9 us
  starting transfers between devices: 56.1 us -> 40.2 us
  other arithmetic: 0 us -> 2.34 us
    unnamed x64 -> x4, local copies, waits for them, and re-layouts: 17.7 us -> 1.04 us
    all_to_all x0 -> x1, blocking collectives: none -> 15.7 us  [on_device(): e_all = lax.all_to_all(msg, PLANE, 0, 0)]
    all_to_all x1 -> x0, starting transfers between devices: 6.03 us -> none  [on_device(): e_all = lax.all_to_all(msg, PLANE, 0, 0)]
    ppermute x8, starting transfers between devices: 13.4 us -> 8.23 us  [pair(): above = lax.ppermute(down_part, axis, down)]
    ppermute x8, starting transfers between devices: 36.7 us -> 32 us  [pair(): below = lax.ppermute(up_part, axis, up)]
    ppermute x8, waiting for transfers between devices: 3.21 us -> 6.62 us  [pair(): below = lax.ppermute(up_part, axis, up)]
    ppermute x8, waiting for transfers between devices: 21.3 us -> 18.4 us  [pair(): above = lax.ppermute(down_part, axis, down)]
  transfers between devices with their start and end apart: 17 -> 16, of which waited for: 11 -> 12; matrix products, arithmetic and copies ran while one was open for 0% -> 0% of each run, Pallas kernels for 0% -> 0%
where the time goes in v3:
time: 169 us; the launch traced here: 168 us
  blocking collectives  90.9 us (54%)
  starting transfers between devices  40.2 us (24%)
  waiting for transfers between devices  25 us (15%)
  Pallas kernels  7.51 us (4%)
  other arithmetic  2.34 us (1%)
    all_to_all x2, blocking collectives, on_device(): got = lax.all_to_all(msg, 'gy', 0, 0)  44.6 us
    ppermute x8, starting transfers between devices, pair(): below = lax.ppermute(up_part, axis, up)  32 us
    all_to_all x2, blocking collectives, on_device(): got = lax.all_to_all(msg, PLANE, 0, 0)  30.6 us
    ppermute x8, waiting for transfers between devices, pair(): above = lax.ppermute(down_part, axis, down)  18.4 us
    all_to_all x1, blocking collectives, on_device(): e_all = lax.all_to_all(msg, PLANE, 0, 0)  15.7 us
    ppermute x8, starting transfers between devices, pair(): above = lax.ppermute(down_part, axis, down)  8.23 us
    pallas_call x13, Pallas kernels, call(): pl.pallas_call(body, out_shape=shapes, in_specs=[pl.BlockSpec(memory_spac...  7.51 us
    ppermute x8, waiting for transfers between devices, pair(): below = lax.ppermute(up_part, axis, up)  6.62 us
  transfers between devices with their start and end apart: 16, of which 12 were waited for; matrix products, arithmetic and copies ran while one was open for 0% of the time, Pallas kernels for 0%

profile of v3, /device:TPU:1, one launch (start us, length us, event | category | flops | bytes accessed | tf_op | source)
XLA Modules:
  0.0 167.9 jit_solution(2346417955578032527)
XLA Ops:
  0.7 0.8 convert_element_type.8
  1.4 0.1 pad.8.clone
  1.5 0.7 fusion
  2.2 0.8 maximum_maximum_fusion.in_ref
  3.0 0.0 copy-start.1
  3.0 1.0 copy-done.1
  4.1 0.6 shard_map.73
  4.7 1.3 collective-permute-start.1
  6.0 4.7 %collective-permute-start = (f32[8,8,128]{2,1,0:T(8,128)S(1)}, f32[8,8,128]{2,1,0:T(8,128)S(1)}, u32[]{:S(2)}, u32[]{:S(2)}) collective-permute-start(f32[8,8,128]{2,1,0:T(8,128)S(1)} %get-tuple-element.48.mine_ref), channel_id=1, source_target_pairs={{0,128},{128,256},{256,384},{1,129},{129,257},{257,385},{2,130},{1... | collective-permute-start | bytes 98312 | tf_op jit(solution)/shard_map/ppermute | solution.py:679
  10.7 0.0 collective-permute-done.1.right_ref.rx_ref.rx
  10.7 1.0 collective-permute-done.left_ref.lx_ref.lx
  11.7 3.7 %collective-permute-start.2 = (f32[48,8,128]{2,1,0:T(8,128)S(1)}, f32[48,8,128]{2,1,0:T(8,128)S(1)}, u32[]{:S(2)}, u32[]{:S(2)}) collective-permute-start(f32[48,8,128]{2,1,0:T(8,128)S(1)} %get-tuple-element.50), channel_id=1, source_target_pairs={{0,8},{8,16},{16,24},{24,32},{32,40},{40,48},{48,56},{56,64},{64,7... | collective-permute-start | bytes 589832 | tf_op jit(solution)/shard_map/ppermute | solution.py:679
  15.4 1.3 collective-permute-start.3
  16.7 1.3 collective-permute-done.2.below_ref.yb_ref.yb
  18.0 4.0 %collective-permute-done.3.above_ref.ya_ref.ya = f32[48,8,128]{2,1,0:T(8,128)S(1)} collective-permute-done((f32[48,8,128]{2,1,0:T(8,128)S(1)}, f32[48,8,128]{2,1,0:T(8,128)S(1)}, u32[]{:S(2)}, u32[]{:S(2)}) %collective-permute-start.3) | collective-permute-done | bytes 196640 | tf_op jit(solution)/shard_map/ppermute | solution.py:680
  22.0 0.1 shard_map.75
  22.1 4.2 %collective-permute-start.4 = (f32[63,8,128]{2,1,0:T(8,128)S(1)}, f32[63,8,128]{2,1,0:T(8,128)S(1)}, u32[]{:S(2)}, u32[]{:S(2)}) collective-permute-start(f32[63,8,128]{2,1,0:T(8,128)S(1)} %get-tuple-element.55), channel_id=1, source_target_pairs={{0,1},{1,2},{2,3},{3,4},{4,5},{5,6},{6,7},{7,0},{8,9},{9,10},{10,1... | collective-permute-start | bytes 774152 | tf_op jit(solution)/shard_map/ppermute | solution.py:679
  26.3 1.7 %collective-permute-start.5 = (f32[63,8,128]{2,1,0:T(8,128)S(1)}, f32[63,8,128]{2,1,0:T(8,128)S(1)}, u32[]{:S(2)}, u32[]{:S(2)}) collective-permute-start(f32[63,8,128]{2,1,0:T(8,128)S(1)} %get-tuple-element.56), channel_id=1, source_target_pairs={{1,0},{2,1},{3,2},{4,3},{5,4},{6,5},{7,6},{0,7},{9,8},{10,9},{11,1... | collective-permute-start | bytes 774152 | tf_op jit(solution)/shard_map/ppermute | solution.py:680
  28.0 1.5 collective-permute-done.4
  29.6 0.0 copy-start
  29.6 2.7 %collective-permute-done.5 = f32[63,8,128]{2,1,0:T(8,128)S(1)} collective-permute-done((f32[63,8,128]{2,1,0:T(8,128)S(1)}, f32[63,8,128]{2,1,0:T(8,128)S(1)}, u32[]{:S(2)}, u32[]{:S(2)}) %collective-permute-start.5) | collective-permute-done | bytes 258080 | tf_op jit(solution)/shard_map/ppermute | solution.py:680
  32.3 2.6 %shard_map.76 = (f32[7,16,16,256]{3,2,1,0:T(8,128)S(1)}, f32[8,8,128]{2,1,0:T(8,128)S(1)}, f32[10,16,256]{2,1,0:T(8,128)S(1)}, f32[16,16,256]{2,1,0:T(8,128)S(1)...) custom-call(f32[5,8,8,128]{3,2,1,0:T(8,128)S(1)} %get-tuple-element.47.f_ref, ...), custom_call_target="tpu_custom_call" | custom-call | tf_op jit(solution)/shard_map/pallas_call | solution.py:22
  34.9 16.3 %all_to_all.25.got_ref = f32[32,8,128]{2,1,0:T(8,128)S(1)} all-to-all(f32[32,8,128]{2,1,0:T(8,128)S(1)} %get-tuple-element.57), channel_id=1, replica_groups=mesh['gx'=4,'gy'=16,'gz'=8] {'gx','gz'}, dimensions={0} | all-to-all | bytes 262144 | tf_op jit(solution)/shard_map/all_to_all | solution.py:716
  51.2 0.1 shard_map.77
  51.3 26.2 %all_to_all.26.got_ref = f32[16,3,8,128]{3,2,1,0:T(8,128)S(1)} all-to-all(f32[16,3,8,128]{3,2,1,0:T(8,128)S(1)} %shard_map.77), channel_id=1, replica_groups=mesh['gx'=4,'gy'=16,'gz'=8] {'gy'}, dimensions={0} | all-to-all | bytes 393216 | tf_op jit(solution)/shard_map/all_to_all | solution.py:718
  77.5 0.0 copy-done
  77.5 0.5 shard_map.78
  78.0 6.5 %collective-permute-start.6 = (f32[4,8,128]{2,1,0:T(8,128)S(1)}, f32[4,8,128]{2,1,0:T(8,128)S(1)}, u32[]{:S(2)}, u32[]{:S(2)}) collective-permute-start(f32[4,8,128]{2,1,0:T(8,128)S(1)} %get-tuple-element.63), channel_id=1, source_target_pairs={{0,8},{8,16},{16,24},{24,32},{32,40},{40,48},{48,56},{56,64},{64,7... | collective-permute-start | bytes 49160 | tf_op jit(solution)/shard_map/ppermute | solution.py:679
  84.6 1.3 collective-permute-start.7
  85.9 0.0 collective-permute-done.6.below_ref
  85.9 3.2 %collective-permute-done.7.above_ref = f32[4,8,128]{2,1,0:T(8,128)S(1)} collective-permute-done((f32[4,8,128]{2,1,0:T(8,128)S(1)}, f32[4,8,128]{2,1,0:T(8,128)S(1)}, u32[]{:S(2)}, u32[]{:S(2)}) %collective-permute-start.7) | collective-permute-done | bytes 16416 | tf_op jit(solution)/shard_map/ppermute | solution.py:680
  89.0 0.1 shard_map.79
  89.1 2.8 %collective-permute-start.8 = (f32[8,8,128]{2,1,0:T(8,128)S(1)}, f32[8,8,128]{2,1,0:T(8,128)S(1)}, u32[]{:S(2)}, u32[]{:S(2)}) collective-permute-start(f32[8,8,128]{2,1,0:T(8,128)S(1)} %get-tuple-element.68), channel_id=1, source_target_pairs={{0,1},{1,2},{2,3},{3,4},{4,5},{5,6},{6,7},{7,0},{8,9},{9,10},{10,1... | collective-permute-start | bytes 98312 | tf_op jit(solution)/shard_map/ppermute | solution.py:679
  91.9 0.0 collective-permute-start.9
  91.9 1.0 collective-permute-done.8
  93.0 2.6 %collective-permute-done.9 = f32[8,8,128]{2,1,0:T(8,128)S(1)} collective-permute-done((f32[8,8,128]{2,1,0:T(8,128)S(1)}, f32[8,8,128]{2,1,0:T(8,128)S(1)}, u32[]{:S(2)}, u32[]{:S(2)}) %collective-permute-start.9) | collective-permute-done | bytes 32800 | tf_op jit(solution)/shard_map/ppermute | solution.py:680
  95.6 15.7 %all_to_all.27.e_ref = f32[32,3,8,128]{3,2,1,0:T(8,128)S(1)} all-to-all(f32[32,3,8,128]{3,2,1,0:T(8,128)S(1)} %get-tuple-element.70), channel_id=1, replica_groups=mesh['gx'=4,'gy'=16,'gz'=8] {'gx','gz'}, dimensions={0} | all-to-all | bytes 786432 | tf_op jit(solution)/shard_map/all_to_all | solution.py:727
  111.3 1.1 shard_map.80
  112.5 1.3 collective-permute-start.11
  113.8 4.0 %collective-permute-start.10 = (f32[1,8,128]{2,1,0:T(8,128)S(1)}, f32[1,8,128]{2,1,0:T(8,128)S(1)}, u32[]{:S(2)}, u32[]{:S(2)}) collective-permute-start(f32[1,8,128]{2,1,0:T(8,128)S(1)} %get-tuple-element.77), channel_id=1, source_target_pairs={{0,128},{128,256},{256,384},{1,129},{129,257},{257,385},{2,130},{1... | collective-permute-start | bytes 12296 | tf_op jit(solution)/shard_map/ppermute | solution.py:679
  117.8 0.0 collective-permute-done.11.right_ref
  117.8 0.7 collective-permute-done.10.left_ref
  118.5 3.0 %collective-permute-start.12 = (f32[5,8,128]{2,1,0:T(8,128)S(1)}, f32[5,8,128]{2,1,0:T(8,128)S(1)}, u32[]{:S(2)}, u32[]{:S(2)}) collective-permute-start(f32[5,8,128]{2,1,0:T(8,128)S(1)} %get-tuple-element.78), channel_id=1, source_target_pairs={{0,8},{8,16},{16,24},{24,32},{32,40},{40,48},{48,56},{56,64},{64,7... | collective-permute-start | bytes 61448 | tf_op jit(solution)/shard_map/ppermute | solution.py:679
  121.5 1.3 collective-permute-start.13
  122.8 0.0 collective-permute-done.12.below_ref
  122.9 3.2 %collective-permute-done.13.above_ref = f32[5,8,128]{2,1,0:T(8,128)S(1)} collective-permute-done((f32[5,8,128]{2,1,0:T(8,128)S(1)}, f32[5,8,128]{2,1,0:T(8,128)S(1)}, u32[]{:S(2)}, u32[]{:S(2)}) %collective-permute-start.13) | collective-permute-done | bytes 20512 | tf_op jit(solution)/shard_map/ppermute | solution.py:680
  126.1 0.1 shard_map.82
  126.1 3.1 %collective-permute-start.14 = (f32[9,8,128]{2,1,0:T(8,128)S(1)}, f32[9,8,128]{2,1,0:T(8,128)S(1)}, u32[]{:S(2)}, u32[]{:S(2)}) collective-permute-start(f32[9,8,128]{2,1,0:T(8,128)S(1)} %get-tuple-element.83), channel_id=1, source_target_pairs={{0,1},{1,2},{2,3},{3,4},{4,5},{5,6},{6,7},{7,0},{8,9},{9,10},{10,1... | collective-permute-start | bytes 110600 | tf_op jit(solution)/shard_map/ppermute | solution.py:679
  129.3 0.0 collective-permute-start.15
  129.3 1.1 collective-permute-done.14
  130.3 2.6 %collective-permute-done.15 = f32[9,8,128]{2,1,0:T(8,128)S(1)} collective-permute-done((f32[9,8,128]{2,1,0:T(8,128)S(1)}, f32[9,8,128]{2,1,0:T(8,128)S(1)}, u32[]{:S(2)}, u32[]{:S(2)}) %collective-permute-start.15) | collective-permute-done | bytes 36896 | tf_op jit(solution)/shard_map/ppermute | solution.py:680
  132.9 0.8 shard_map.83
  133.8 14.4 %all_to_all.28.got_ref = f32[32,8,128]{2,1,0:T(8,128)S(1)} all-to-all(f32[32,8,128]{2,1,0:T(8,128)S(1)} %get-tuple-element.85), channel_id=1, replica_groups=mesh['gx'=4,'gy'=16,'gz'=8] {'gx','gz'}, dimensions={0} | all-to-all | bytes 262144 | tf_op jit(solution)/shard_map/all_to_all | solution.py:740
  148.1 0.1 shard_map.84
  148.2 18.3 %all_to_all.29.got_ref = f32[16,8,128]{2,1,0:T(8,128)S(1)} all-to-all(f32[16,8,128]{2,1,0:T(8,128)S(1)} %shard_map.84), channel_id=1, replica_groups=mesh['gx'=4,'gy'=16,'gz'=8] {'gy'}, dimensions={0} | all-to-all | bytes 131072 | tf_op jit(solution)/shard_map/all_to_all | solution.py:742
  166.5 1.4 shard_map.85
  (8 shorter events, 0.1 us)
Async XLA Ops:
  3.0 1.0 copy-start.1
  4.7 6.0 %collective-permute-start.1 = (f32[8,8,128]{2,1,0:T(8,128)S(1)}, f32[8,8,128]{2,1,0:T(8,128)S(1)}, u32[]{:S(2)}, u32[]{:S(2)}) collective-permute-start(f32[8,8,128]{2,1,0:T(8,128)S(1)} %get-tuple-element.48.mine_ref), channel_id=1, source_target_pairs={{128,0},{256,128},{384,256},{129,1},{257,129},{385,257},{130,2},{2... | collective-permute-start | bytes 98312 | tf_op jit(solution)/shard_map/ppermute | solution.py:680
  6.0 5.7 %collective-permute-start = (f32[8,8,128]{2,1,0:T(8,128)S(1)}, f32[8,8,128]{2,1,0:T(8,128)S(1)}, u32[]{:S(2)}, u32[]{:S(2)}) collective-permute-start(f32[8,8,128]{2,1,0:T(8,128)S(1)} %get-tuple-element.48.mine_ref), channel_id=1, source_target_pairs={{0,128},{128,256},{256,384},{1,129},{129,257},{257,385},{2,130},{1... | collective-permute-start | bytes 98312 | tf_op jit(solution)/shard_map/ppermute | solution.py:679
  11.7 6.3 %collective-permute-start.2 = (f32[48,8,128]{2,1,0:T(8,128)S(1)}, f32[48,8,128]{2,1,0:T(8,128)S(1)}, u32[]{:S(2)}, u32[]{:S(2)}) collective-permute-start(f32[48,8,128]{2,1,0:T(8,128)S(1)} %get-tuple-element.50), channel_id=1, source_target_pairs={{0,8},{8,16},{16,24},{24,32},{32,40},{40,48},{48,56},{56,64},{64,7... | collective-permute-start | bytes 589832 | tf_op jit(solution)/shard_map/ppermute | solution.py:679
  15.4 6.6 %collective-permute-start.3 = (f32[48,8,128]{2,1,0:T(8,128)S(1)}, f32[48,8,128]{2,1,0:T(8,128)S(1)}, u32[]{:S(2)}, u32[]{:S(2)}) collective-permute-start(f32[48,8,128]{2,1,0:T(8,128)S(1)} %get-tuple-element.51), channel_id=1, source_target_pairs={{8,0},{16,8},{24,16},{32,24},{40,32},{48,40},{56,48},{64,56},{72,6... | collective-permute-start | bytes 589832 | tf_op jit(solution)/shard_map/ppermute | solution.py:680
  22.1 7.4 %collective-permute-start.4 = (f32[63,8,128]{2,1,0:T(8,128)S(1)}, f32[63,8,128]{2,1,0:T(8,128)S(1)}, u32[]{:S(2)}, u32[]{:S(2)}) collective-permute-start(f32[63,8,128]{2,1,0:T(8,128)S(1)} %get-tuple-element.55), channel_id=1, source_target_pairs={{0,1},{1,2},{2,3},{3,4},{4,5},{5,6},{6,7},{7,0},{8,9},{9,10},{10,1... | collective-permute-start | bytes 774152 | tf_op jit(solution)/shard_map/ppermute | solution.py:679
  26.3 6.0 %collective-permute-start.5 = (f32[63,8,128]{2,1,0:T(8,128)S(1)}, f32[63,8,128]{2,1,0:T(8,128)S(1)}, u32[]{:S(2)}, u32[]{:S(2)}) collective-permute-start(f32[63,8,128]{2,1,0:T(8,128)S(1)} %get-tuple-element.56), channel_id=1, source_target_pairs={{1,0},{2,1},{3,2},{4,3},{5,4},{6,5},{7,6},{0,7},{9,8},{10,9},{11,1... | collective-permute-start | bytes 774152 | tf_op jit(solution)/shard_map/ppermute | solution.py:680
  29.6 48.0 %copy-start = (f32[256,256]{1,0:T(8,128)S(1)}, f32[256,256]{1,0:T(8,128)}, u32[]{:S(2)}) copy-start(f32[256,256]{1,0:T(8,128)} %cinv_ref.5) | copy-start | bytes 786436
  78.0 7.8 %collective-permute-start.6 = (f32[4,8,128]{2,1,0:T(8,128)S(1)}, f32[4,8,128]{2,1,0:T(8,128)S(1)}, u32[]{:S(2)}, u32[]{:S(2)}) collective-permute-start(f32[4,8,128]{2,1,0:T(8,128)S(1)} %get-tuple-element.63), channel_id=1, source_target_pairs={{0,8},{8,16},{16,24},{24,32},{32,40},{40,48},{48,56},{56,64},{64,7... | collective-permute-start | bytes 49160 | tf_op jit(solution)/shard_map/ppermute | solution.py:679
  84.6 4.5 %collective-permute-start.7 = (f32[4,8,128]{2,1,0:T(8,128)S(1)}, f32[4,8,128]{2,1,0:T(8,128)S(1)}, u32[]{:S(2)}, u32[]{:S(2)}) collective-permute-start(f32[4,8,128]{2,1,0:T(8,128)S(1)} %get-tuple-element.64), channel_id=1, source_target_pairs={{8,0},{16,8},{24,16},{32,24},{40,32},{48,40},{56,48},{64,56},{72,6... | collective-permute-start | bytes 49160 | tf_op jit(solution)/shard_map/ppermute | solution.py:680
  89.1 3.8 %collective-permute-start.8 = (f32[8,8,128]{2,1,0:T(8,128)S(1)}, f32[8,8,128]{2,1,0:T(8,128)S(1)}, u32[]{:S(2)}, u32[]{:S(2)}) collective-permute-start(f32[8,8,128]{2,1,0:T(8,128)S(1)} %get-tuple-element.68), channel_id=1, source_target_pairs={{0,1},{1,2},{2,3},{3,4},{4,5},{5,6},{6,7},{7,0},{8,9},{9,10},{10,1... | collective-permute-start | bytes 98312 | tf_op jit(solution)/shard_map/ppermute | solution.py:679
  91.9 3.6 %collective-permute-start.9 = (f32[8,8,128]{2,1,0:T(8,128)S(1)}, f32[8,8,128]{2,1,0:T(8,128)S(1)}, u32[]{:S(2)}, u32[]{:S(2)}) collective-permute-start(f32[8,8,128]{2,1,0:T(8,128)S(1)} %get-tuple-element.69), channel_id=1, source_target_pairs={{1,0},{2,1},{3,2},{4,3},{5,4},{6,5},{7,6},{0,7},{9,8},{10,9},{11,1... | collective-permute-start | bytes 98312 | tf_op jit(solution)/shard_map/ppermute | solution.py:680
  112.5 5.3 %collective-permute-start.11 = (f32[1,8,128]{2,1,0:T(8,128)S(1)}, f32[1,8,128]{2,1,0:T(8,128)S(1)}, u32[]{:S(2)}, u32[]{:S(2)}) collective-permute-start(f32[1,8,128]{2,1,0:T(8,128)S(1)} %get-tuple-element.77), channel_id=1, source_target_pairs={{128,0},{256,128},{384,256},{129,1},{257,129},{385,257},{130,2},{2... | collective-permute-start | bytes 12296 | tf_op jit(solution)/shard_map/ppermute | solution.py:680
  113.8 4.7 %collective-permute-start.10 = (f32[1,8,128]{2,1,0:T(8,128)S(1)}, f32[1,8,128]{2,1,0:T(8,128)S(1)}, u32[]{:S(2)}, u32[]{:S(2)}) collective-permute-start(f32[1,8,128]{2,1,0:T(8,128)S(1)} %get-tuple-element.77), channel_id=1, source_target_pairs={{0,128},{128,256},{256,384},{1,129},{129,257},{257,385},{2,130},{1... | collective-permute-start | bytes 12296 | tf_op jit(solution)/shard_map/ppermute | solution.py:679
  118.5 4.3 %collective-permute-start.12 = (f32[5,8,128]{2,1,0:T(8,128)S(1)}, f32[5,8,128]{2,1,0:T(8,128)S(1)}, u32[]{:S(2)}, u32[]{:S(2)}) collective-permute-start(f32[5,8,128]{2,1,0:T(8,128)S(1)} %get-tuple-element.78), channel_id=1, source_target_pairs={{0,8},{8,16},{16,24},{24,32},{32,40},{40,48},{48,56},{56,64},{64,7... | collective-permute-start | bytes 61448 | tf_op jit(solution)/shard_map/ppermute | solution.py:679
  121.5 4.5 %collective-permute-start.13 = (f32[5,8,128]{2,1,0:T(8,128)S(1)}, f32[5,8,128]{2,1,0:T(8,128)S(1)}, u32[]{:S(2)}, u32[]{:S(2)}) collective-permute-start(f32[5,8,128]{2,1,0:T(8,128)S(1)} %get-tuple-element.79), channel_id=1, source_target_pairs={{8,0},{16,8},{24,16},{32,24},{40,32},{48,40},{56,48},{64,56},{72,6... | collective-permute-start | bytes 61448 | tf_op jit(solution)/shard_map/ppermute | solution.py:680
  126.1 4.2 %collective-permute-start.14 = (f32[9,8,128]{2,1,0:T(8,128)S(1)}, f32[9,8,128]{2,1,0:T(8,128)S(1)}, u32[]{:S(2)}, u32[]{:S(2)}) collective-permute-start(f32[9,8,128]{2,1,0:T(8,128)S(1)} %get-tuple-element.83), channel_id=1, source_target_pairs={{0,1},{1,2},{2,3},{3,4},{4,5},{5,6},{6,7},{7,0},{8,9},{9,10},{10,1... | collective-permute-start | bytes 110600 | tf_op jit(solution)/shard_map/ppermute | solution.py:679
  129.3 3.7 %collective-permute-start.15 = (f32[9,8,128]{2,1,0:T(8,128)S(1)}, f32[9,8,128]{2,1,0:T(8,128)S(1)}, u32[]{:S(2)}, u32[]{:S(2)}) collective-permute-start(f32[9,8,128]{2,1,0:T(8,128)S(1)} %get-tuple-element.84), channel_id=1, source_target_pairs={{1,0},{2,1},{3,2},{4,3},{5,4},{6,5},{7,6},{0,7},{9,8},{10,9},{11,1... | collective-permute-start | bytes 110600 | tf_op jit(solution)/shard_map/ppermute | solution.py:680
